TPU v7x, 32 devices: a whole 2x2x4 slice. The times are simulated.
32 devices in a mesh: group: 2 (over x), sector: 16 (over z, y, core).
Axes of the slice: x: 2, y: 2, z: 4, core: 2. Of those that a mesh axis runs over, the one named last changes fastest.
Arguments:
- field: float32 [4, 5, 16, 16, 4096], P('group', None, None, 'sector'), parts along dimension 0, may hold values from -6 to 6
- axial_jac: float32 [2, 5, 5], replicated, may hold values from -2.5 to 2.5
- circ_jac: float32 [2, 5, 5], replicated, may hold values from -2.5 to 2.5
- left_char: float32 [2, 5, 5], replicated, may hold values from -2.5 to 2.5
- right_char: float32 [2, 5, 5], replicated, may hold values from -2.5 to 2.5
- mode_source: int32 [2, 256], replicated, may hold values from 0 to 255, as said below
- mode_target: int32 [2, 256], replicated, may hold values from 0 to 255, as said below
- mode_count: int32 [2], replicated, may hold values from 128 to 256, as said below
- section_offset: int32 [4], replicated, may hold values from 0 to 511
Outputs:
- advanced: float32 [4, 5, 16, 16, 4096], P('group', None, None, 'sector'), parts along dimension 0
There are 2 independent parts, one for each index of `group`. A program takes and returns all parts, laid end to end along the dimension named above; an argument that names none is the same for every part. Nothing has to cross between parts.
Inputs may be any that keep to these rules, and one draw needn't show every extreme that they name: `mode_source`: each row is a permutation of 0 to 255; entries at pair index mode_count[d] or beyond are padding. `mode_target`: each row is a permutation of 0 to 255; entries at pair index mode_count[d] or beyond are padding. `mode_count`: the first direction's count is 256.
All inputs are finite; a program needn't handle non-finite values.
Results may differ from a plain program's by a relative error of at most 0.00005.
Values sent between devices are 32-bit elements; how exact they have to be, the bound alone decides.
A program may use at most 128 MiB of HBM per device.

v0:
```python
import math

import jax
import jax.numpy as jnp
from jax import lax
from jax.sharding import PartitionSpec as P

NTH = 512
VARS = 5
NB = 8
NR = 128
K = 256


precise = lax.Precision.HIGHEST
time_step = 0.2
diffusion = 0.05


def passed_along(block, axis, distance):
    devices = range(lax.axis_size(axis))
    route = [((i - distance) % len(devices), i) for i in devices]
    return lax.ppermute(block, axis, route)


def with_halo(x, sides, width):
    for axis, dim in sides:
        size, length = (lax.axis_size(axis), x.shape[dim])
        up = [(i, (i + 1) % size) for i in range(size)]
        down = [(j, i) for i, j in up]
        last = lax.slice_in_dim(x, length - width, length, axis=dim)
        first = lax.slice_in_dim(x, 0, width, axis=dim)
        before = lax.ppermute(last, axis, up)
        after = lax.ppermute(first, axis, down)
        x = jnp.concatenate([before, x, after], axis=dim)
    return x


def fourier_tables():
    theta = jnp.arange(NTH, dtype=jnp.int32)
    modes = jnp.arange(K, dtype=jnp.int32)
    phase = (theta[:, None] * modes[None, :] % NTH).astype(jnp.float32) * (2.0 * math.pi / NTH)
    cosine = jnp.cos(phase)
    sine = jnp.sin(phase)
    forward = jnp.concatenate([cosine, -sine], axis=1)
    weights = jnp.where(modes == 0, 1.0 / NTH, 2.0 / NTH).astype(jnp.float32)
    inverse = jnp.concatenate([(cosine * weights[None, :]).T, -(sine * weights[None, :]).T], axis=0)
    return (forward, inverse)


def matching(source, target, count, offset, sign):
    modes = jnp.arange(K, dtype=jnp.int32)
    valid = (modes < count).astype(jnp.float32)
    phase = (source * offset % NTH).astype(jnp.float32) * (sign * 2.0 * math.pi / NTH)
    weighted_cos = jnp.cos(phase) * valid
    weighted_sin = jnp.sin(phase) * valid
    one_source = (source[:, None] == modes[None, :]).astype(jnp.float32)
    one_target = (target[:, None] == modes[None, :]).astype(jnp.float32)
    keep = jnp.dot(one_source.T, weighted_cos[:, None] * one_target, precision=precise)
    turn = jnp.dot(one_source.T, weighted_sin[:, None] * one_target, precision=precise)
    return jnp.concatenate([jnp.concatenate([keep, turn], 1), jnp.concatenate([-turn, keep], 1)], 0)


def transform(planes, left_char, right_char, mats, forward, inverse):
    spectrum = jnp.einsum("dvrt,tk->dvrk", planes, forward, precision=precise)
    charac = jnp.einsum("dwv,dvrk->dwrk", left_char, spectrum, precision=precise)
    moved = jnp.einsum("dwrk,dkm->dwrm", charac, mats, precision=precise)
    back = jnp.einsum("dvw,dwrm->dvrm", right_char, moved, precision=precise)
    return jnp.einsum("dvrm,mt->dvrt", back, inverse, precision=precise)


def stencil(state, cycle, radial, ghosts, axial_jac, circ_jac):
    zero = jnp.zeros_like(ghosts[0])
    lower = jnp.stack([zero, ghosts[0]])
    upper = jnp.stack([ghosts[1], zero])
    axial = jnp.concatenate([lower[:, :, None], state, upper[:, :, None]], axis=2)
    d_axial = (axial[:, :, 2:] - axial[:, :, :-2]) * 0.5
    d_circ = (cycle[:, :, :, 2:] - cycle[:, :, :, :-2]) * 0.5
    neighbours = axial[:, :, 2:] + axial[:, :, :-2] + cycle[:, :, :, 2:] + cycle[:, :, :, :-2]
    neighbours = neighbours + radial[..., 2:] + radial[..., :-2]
    flux = jnp.einsum("rvw,rwatn->rvatn", axial_jac, d_axial, precision=precise)
    flux = flux + jnp.einsum("rvw,rwatn->rvatn", circ_jac, d_circ, precision=precise)
    return -flux + diffusion * (neighbours - 6.0 * state)


def on_device(
    field,
    axial_jac,
    circ_jac,
    left_char,
    right_char,
    mode_source,
    mode_target,
    mode_count,
    section_offset,
):
    forward, inverse = fourier_tables()
    devices = lax.axis_size("sector")
    index = lax.axis_index("sector")
    depth = field.shape[2]
    rows = NR // NB
    slots = field.shape[4] // rows
    sectors = devices // NB
    per_band = devices // NB
    owned = NR // devices
    half_band = NB // 2
    position = (index + half_band) % devices
    band = position % NB
    cell_band = index // per_band
    low_keep = (band > 0).astype(jnp.float32)
    high_keep = (band < NB - 1).astype(jnp.float32)
    grid = field.reshape(2, VARS, depth, slots, rows)

    def rates(state, offset):
        mats = jnp.stack(
            [
                matching(mode_source[0], mode_target[0], mode_count[0], offset, 1.0),
                matching(mode_source[1], mode_target[1], mode_count[1], offset, -1.0),
            ]
        )
        planes = jnp.stack([state[0, :, -1], state[1, :, 0]])
        outgoing = jnp.transpose(planes.reshape(2, VARS, slots, per_band, owned), (3, 0, 1, 2, 4))
        buffer = jnp.zeros((devices, 2, VARS, slots, owned), jnp.float32)
        buffer = lax.dynamic_update_slice_in_dim(buffer, outgoing, band * per_band, 0)
        arrived = lax.all_to_all(buffer, "sector", split_axis=0, concat_axis=0, tiled=True)
        arrived = jnp.roll(arrived, half_band, axis=0).reshape(sectors, NB, 2, VARS, slots, owned)
        picked = lax.dynamic_index_in_dim(arrived, cell_band, 1, keepdims=False)
        banded = jnp.transpose(picked, (1, 2, 4, 0, 3)).reshape(2, VARS, owned, sectors * slots)
        band_ghosts = transform(banded, left_char, right_char, mats, forward, inverse)
        reply = jnp.transpose(band_ghosts.reshape(2, VARS, owned, sectors, slots), (3, 0, 1, 4, 2))
        back = jnp.zeros((sectors, NB, 2, VARS, slots, owned), jnp.float32)
        back = lax.dynamic_update_index_in_dim(back, reply, cell_band, 1)
        back = jnp.roll(back.reshape(devices, 2, VARS, slots, owned), -half_band, axis=0)
        returned = lax.all_to_all(back, "sector", split_axis=0, concat_axis=0, tiled=True)
        mine = lax.dynamic_slice_in_dim(returned, band * per_band, per_band, 0)
        ghosts = jnp.transpose(mine, (1, 2, 3, 0, 4)).reshape(2, VARS, slots, rows)
        before = passed_along(state[:, :, :, -1:], "sector", NB)
        after = passed_along(state[:, :, :, :1], "sector", -NB)
        cycle = jnp.concatenate([before, state, after], axis=3)
        widened = with_halo(state, (("sector", 4),), 1)
        radial = jnp.concatenate(
            [widened[..., :1] * low_keep, widened[..., 1:-1], widened[..., -1:] * high_keep], axis=4
        )
        return stencil(state, cycle, radial, ghosts, axial_jac, circ_jac)

    first = rates(grid, section_offset[0])
    second = rates(grid + 0.5 * time_step * first, section_offset[1])
    third = rates(grid + 0.5 * time_step * second, section_offset[2])
    fourth = rates(grid + time_step * third, section_offset[3])
    result = grid + time_step / 6.0 * (first + 2.0 * second + 2.0 * third + fourth)
    return result.reshape(field.shape)


def solution(mesh):
    in_specs = (P("group", None, None, "sector", None), P(), P(), P(), P(), P(), P(), P(), P())
    out_specs = P("group", None, None, "sector", None)
    return jax.shard_map(
        on_device, mesh=mesh, in_specs=in_specs, out_specs=out_specs, check_vma=False
    )
```

profile of v0, /device:TPU:0, one launch (start us, length us, event | category | flops | bytes accessed | tf_op | source)
XLA Modules:
  0.0 592.9 jit_solution(12082086075327294219)
XLA Ops:
  0.0 8.6 %reduce = f32[2,5,16,4096]{3,2,1,0:T(8,128)S(1)} reduce(f32[2,5,16,1,4096]{4,3,2,1,0:T(1,128)} %param.9, f32[]{:T(128)} %constant.201), dimensions={3}, to_apply=%param.9.reduce_sub_computation | reduce | bytes 5242884 | tf_op args[0]
  8.6 11.1 %reshape.331 = f32[2,5,16,256,16]{4,3,2,1,0:T(8,128)} reshape(f32[2,5,16,4096]{3,2,1,0:T(8,128)S(1)} %reduce) | data formatting | bytes 5242880 | tf_op jit(solution)/shard_map/reshape | solution.py:112
  23.5 7.6 %all-to-all-start = ((f32[16,2,5,256,8]{3,4,2,1,0:T(8,128)}), f32[16,2,5,256,8]{3,4,2,1,0:T(8,128)S(1)}, u32[]{:S(2)}, u32[]{:S(2)}) async-start(f32[16,2,5,256,8]{3,4,2,1,0:T(8,128)} %copy_dynamic-update-slice_fusion.4), calls=%async_computation | async-start | bytes 2621440 | tf_op jit(solution)/shard_map/all_to_all | solution.py:125
  31.1 2.1 sine_negate_fusion
  34.4 3.8 sine_select_fusion.1
  41.5 3.8 sine_select_fusion
  48.1 2.1 cosine_multiply_fusion
  50.2 8.3 %all-to-all-done = f32[16,2,5,256,8]{3,4,2,1,0:T(8,128)S(1)} async-done(((f32[16,2,5,256,8]{3,4,2,1,0:T(8,128)}), f32[16,2,5,256,8]{3,4,2,1,0:T(8,128)S(1)}, u32[]{:S(2)}, u32[]{:S(2)}) %all-to-all-start) | async-done | bytes 1310752 | tf_op jit(solution)/shard_map/all_to_all | solution.py:125
  61.9 3.4 fusion.49
  68.0 8.4 %all-to-all-start.1 = ((f32[16,2,5,256,8]{3,4,2,1,0:T(8,128)}), f32[16,2,5,256,8]{3,4,2,1,0:T(8,128)S(1)}, u32[]{:S(2)}, u32[]{:S(2)}) async-start(f32[16,2,5,256,8]{3,4,2,1,0:T(8,128)} %pad_maximum_fusion.37), calls=%async_computation.1 | async-start | bytes 2621440 | tf_op jit(solution)/shard_map/all_to_all | solution.py:134
  76.4 14.4 %copy.253 = f32[2,5,16,256,16]{3,1,4,2,0:T(8,128)} copy(f32[2,5,16,256,16]{4,3,2,1,0:T(8,128)} %reshape.331) | data formatting | bytes 5242880 | tf_op jit(solution)/shard_map/reshape | solution.py:112
  92.7 4.5 collective-permute-start.2
  97.2 2.1 fusion.295
  99.3 2.9 collective-permute-start.1
  102.2 15.5 %collective-permute-done = f32[2,5,16,1,16]{4,2,3,1,0:T(8,128)} collective-permute-done((f32[2,5,16,1,16]{4,2,3,1,0:T(8,128)}, f32[2,5,16,1,16]{4,2,3,1,0:T(8,128)}, u32[]{:S(2)}, u32[]{:S(2)}) %collective-permute-start) | collective-permute-done | bytes 10272 | tf_op jit(solution)/shard_map/ppermute | solution.py:23
  117.7 3.2 copy.189
  120.9 2.3 copy.191
  126.8 7.4 %fusion.47 = f32[2,16,256,16,5]{2,4,3,1,0:T(8,128)S(1)} fusion(f32[2,5,16,256,16]{3,1,4,2,0:T(8,128)} %copy.253, f32[2,5,1,256,16]{3,1,4,2,0:T(8,128)S(1)} %pad_bitcast_fusion.6, f32[2,5,1,256,16]{3,1,4,2,0:T(8,128)S(1)} %pad_bitcast_fusion.7, f32[2,5,5,1,1]{2,0,1,4,3:T(2,128)S(1)} %bitcast.279), kind=kOutput, calls=%fused_computation.73 | convolution fusion | flops 41943040 | bytes 5570760 | tf_op jit(solution)/shard_map/rvw,rwatn->rvatn/dot_general | solution.py:81
  134.3 12.0 %multiply_add_fusion.2 = (f32[2,5,16,256,16]{3,1,4,2,0:T(8,128)S(1)}, f32[2,16,256,16,5]{2,4,3,1,0:T(8,128)}) fusion(f32[2,5,16,256,16]{3,1,4,2,0:T(8,128)S(1)} %copy-done.5, f32[2,5,16,256,1]{3,1,4,2,0:T(8,128)S(1)} %copy-done.16, f32[2,5,16,256,1]{3,1,4,2,0:T(8,128)S(1)} %copy-done.15, f32[2,5,1,256,16]{3,1,4,2,0:T(8,128)S(1)} %pad_bitcast_fusion.7, ...), kind=kOutput, calls=%fused_computation.67 | convolution fusion | flops 54394880 | bytes 11161800 | tf_op jit(solution)/shard_map/rvw,rwatn->rvatn/dot_general | solution.py:82
  146.3 2.0 copy-done.4
  150.3 3.9 all-to-all-start.2
  159.2 22.3 %all-to-all-done.2 = f32[16,2,5,256,8]{3,4,2,1,0:T(8,128)S(1)} async-done(((f32[16,2,5,256,8]{3,4,2,1,0:T(8,128)}), f32[16,2,5,256,8]{3,4,2,1,0:T(8,128)S(1)}, u32[]{:S(2)}, u32[]{:S(2)}) %all-to-all-start.2) | async-done | bytes 1310752 | tf_op jit(solution)/shard_map/all_to_all | solution.py:125
  185.0 3.4 fusion.52
  191.0 8.0 %all-to-all-start.3 = ((f32[16,2,5,256,8]{3,4,2,1,0:T(8,128)}), f32[16,2,5,256,8]{3,4,2,1,0:T(8,128)S(1)}, u32[]{:S(2)}, u32[]{:S(2)}) async-start(f32[16,2,5,256,8]{3,4,2,1,0:T(8,128)} %pad_maximum_fusion.39), calls=%async_computation.3 | async-start | bytes 2621440 | tf_op jit(solution)/shard_map/all_to_all | solution.py:134
  199.0 4.9 fusion.304
  203.9 2.6 copy.212
  206.5 2.9 collective-permute-start.4
  209.4 3.2 copy.214
  214.6 3.8 collective-permute-start.6
  218.6 18.5 %collective-permute-done.4 = f32[2,5,16,1,16]{4,2,3,1,0:T(8,128)} collective-permute-done((f32[2,5,16,1,16]{4,2,3,1,0:T(8,128)S(1)}, f32[2,5,16,1,16]{4,2,3,1,0:T(8,128)}, u32[]{:S(2)}, u32[]{:S(2)}) %collective-permute-start.4) | collective-permute-done | bytes 10272 | tf_op jit(solution)/shard_map/ppermute | solution.py:23
  237.1 3.2 copy.213
  240.3 3.2 copy.215
  243.5 12.3 %fusion.35 = f32[2,16,256,16,5]{2,4,3,1,0:T(8,128)} fusion(f32[2,5,16,1,16]{3,1,4,2,0:T(8,128)} %copy.213, f32[2,5,16,256,16]{3,1,4,2,0:T(8,128)} %copy-done.4, f32[2,5,16,1,16]{3,1,4,2,0:T(8,128)} %copy.215, f32[2,5,5,1,1]{2,0,1,4,3:T(2,128)S(1)} %bitcast.238), kind=kOutput, calls=%fused_computation.61 | convolution fusion | flops 41943040 | bytes 5263560 | tf_op jit(solution)/shard_map/rvw,rwatn->rvatn/dot_general | solution.py:82
  259.4 27.1 %multiply_add_fusion.1 = (f32[2,5,16,256,16]{3,1,4,2,0:T(8,128)S(1)}, f32[2,5,16,256,16]{3,1,4,2,0:T(8,128)}) fusion(f32[2,5,16,256,16]{3,1,4,2,0:T(8,128)} %copy.253, f32[2,5,16,256,16]{3,1,4,2,0:T(8,128)} %copy-done.4, f32[2,5,16,256,1]{3,1,4,2,0:T(8,128)} %broadcast_multiply_fusion.2, f32[2,5,16,256,1]{3,1,4,2,0:T(8,128)} %broadcast_multiply_fusion.6, ...), kind=kOutput, calls=%fused_computation.60 | convolution fusion | flops 54394880 | bytes 13783240 | tf_op jit(solution)/shard_map/rvw,rwatn->rvatn/dot_general | solution.py:81
  286.5 2.0 copy-done.1
  290.4 6.1 %all-to-all-start.4 = ((f32[16,2,5,256,8]{3,4,2,1,0:T(8,128)}), f32[16,2,5,256,8]{3,4,2,1,0:T(8,128)S(1)}, u32[]{:S(2)}, u32[]{:S(2)}) async-start(f32[16,2,5,256,8]{3,4,2,1,0:T(8,128)} %fusion.129), calls=%async_computation.4 | async-start | bytes 2621440 | tf_op jit(solution)/shard_map/all_to_all | solution.py:125
  302.7 21.2 %all-to-all-done.4 = f32[16,2,5,256,8]{3,4,2,1,0:T(8,128)S(1)} async-done(((f32[16,2,5,256,8]{3,4,2,1,0:T(8,128)}), f32[16,2,5,256,8]{3,4,2,1,0:T(8,128)S(1)}, u32[]{:S(2)}, u32[]{:S(2)}) %all-to-all-start.4) | async-done | bytes 1310752 | tf_op jit(solution)/shard_map/all_to_all | solution.py:125
  327.4 3.4 fusion.55
  333.5 8.0 %all-to-all-start.5 = ((f32[16,2,5,256,8]{3,4,2,1,0:T(8,128)}), f32[16,2,5,256,8]{3,4,2,1,0:T(8,128)S(1)}, u32[]{:S(2)}, u32[]{:S(2)}) async-start(f32[16,2,5,256,8]{3,4,2,1,0:T(8,128)} %pad_maximum_fusion.41), calls=%async_computation.5 | async-start | bytes 2621440 | tf_op jit(solution)/shard_map/all_to_all | solution.py:134
  343.3 4.4 collective-permute-start.10
  347.7 4.9 fusion.300
  352.6 2.6 copy.230
  355.3 3.2 copy.232
  358.5 2.9 collective-permute-start.9
  361.5 21.2 %collective-permute-done.8 = f32[2,5,16,1,16]{4,2,3,1,0:T(8,128)} collective-permute-done((f32[2,5,16,1,16]{4,2,3,1,0:T(8,128)S(1)}, f32[2,5,16,1,16]{4,2,3,1,0:T(8,128)}, u32[]{:S(2)}, u32[]{:S(2)}) %collective-permute-start.8) | collective-permute-done | bytes 10272 | tf_op jit(solution)/shard_map/ppermute | solution.py:23
  382.7 3.2 copy.231
  386.0 3.2 copy.233
  392.7 7.4 %fusion.32 = f32[2,16,256,16,5]{2,4,3,1,0:T(8,128)S(1)} fusion(f32[2,5,1,256,16]{3,1,4,2,0:T(8,128)S(1)} %pad_bitcast_fusion.3, f32[2,5,16,256,16]{3,1,4,2,0:T(8,128)} %copy-done.1, f32[2,5,1,256,16]{3,1,4,2,0:T(8,128)S(1)} %pad_bitcast_fusion.2, f32[2,5,5,1,1]{2,0,1,4,3:T(2,128)S(1)} %bitcast.281), kind=kOutput, calls=%fused_computation.57 | convolution fusion | flops 41943040 | bytes 5570760 | tf_op jit(solution)/shard_map/rvw,rwatn->rvatn/dot_general | solution.py:81
  400.2 14.8 %multiply_add_fusion = (f32[2,5,16,256,16]{3,1,4,2,0:T(8,128)S(1)}, f32[2,5,16,256,16]{3,1,4,2,0:T(8,128)}) fusion(f32[2,5,16,256,16]{3,1,4,2,0:T(8,128)S(1)} %copy-done.6, f32[2,5,16,256,16]{3,1,4,2,0:T(8,128)S(1)} %copy-done.2, f32[2,5,16,256,1]{3,1,4,2,0:T(8,128)S(1)} %copy-done.18, f32[2,5,16,256,1]{3,1,4,2,0:T(8,128)S(1)} %copy-done.17, ...), kind=kOutput, calls=%fused_computation.53 | convolution fusion | flops 54394880 | bytes 13783240 | tf_op jit(solution)/shard_map/rvw,rwatn->rvatn/dot_general | solution.py:82
  415.1 2.1 copy-done.3
  419.1 3.9 all-to-all-start.6
  428.0 22.4 %all-to-all-done.6 = f32[16,2,5,256,8]{3,4,2,1,0:T(8,128)S(1)} async-done(((f32[16,2,5,256,8]{3,4,2,1,0:T(8,128)}), f32[16,2,5,256,8]{3,4,2,1,0:T(8,128)S(1)}, u32[]{:S(2)}, u32[]{:S(2)}) %all-to-all-start.6) | async-done | bytes 1310752 | tf_op jit(solution)/shard_map/all_to_all | solution.py:125
  453.8 3.4 fusion.58
  459.8 8.0 %all-to-all-start.7 = ((f32[16,2,5,256,8]{3,4,2,1,0:T(8,128)}), f32[16,2,5,256,8]{3,4,2,1,0:T(8,128)S(1)}, u32[]{:S(2)}, u32[]{:S(2)}) async-start(f32[16,2,5,256,8]{3,4,2,1,0:T(8,128)} %pad_maximum_fusion.43), calls=%async_computation.7 | async-start | bytes 2621440 | tf_op jit(solution)/shard_map/all_to_all | solution.py:134
  467.8 4.3 fusion.298
  472.1 2.6 copy.248
  474.7 2.9 collective-permute-start.12
  481.2 3.8 collective-permute-start.14
  485.3 20.6 %collective-permute-done.12 = f32[2,5,16,1,16]{4,2,3,1,0:T(8,128)} collective-permute-done((f32[2,5,16,1,16]{4,2,3,1,0:T(8,128)S(1)}, f32[2,5,16,1,16]{4,2,3,1,0:T(8,128)}, u32[]{:S(2)}, u32[]{:S(2)}) %collective-permute-start.12) | collective-permute-done | bytes 10272 | tf_op jit(solution)/shard_map/ppermute | solution.py:23
  507.8 3.2 copy.251
  511.0 11.9 %fusion.23 = f32[2,16,256,16,5]{2,4,3,1,0:T(8,128)} fusion(f32[2,5,16,1,16]{3,1,4,2,0:T(8,128)S(1)} %copy.249, f32[2,5,16,256,16]{3,1,4,2,0:T(8,128)} %copy-done.3, f32[2,5,16,1,16]{3,1,4,2,0:T(8,128)} %copy.251, f32[2,5,5,1,1]{2,0,1,4,3:T(2,128)S(1)} %bitcast.236), kind=kOutput, calls=%fused_computation.47 | convolution fusion | flops 41943040 | bytes 5263560 | tf_op jit(solution)/shard_map/rvw,rwatn->rvatn/dot_general | solution.py:82
  526.5 39.3 %fusion.6 = f32[2,5,16,256,16]{3,1,4,2,0:T(8,128)} fusion(f32[2,5,16,256,16]{3,1,4,2,0:T(8,128)} %copy.253, f32[2,5,16,256,16]{3,1,4,2,0:T(8,128)} %copy-done.3, f32[2,5,16,256,1]{3,1,4,2,0:T(8,128)} %broadcast_multiply_fusion, f32[2,5,16,256,1]{3,1,4,2,0:T(8,128)} %broadcast_multiply_fusion.4, f32[2,16,256,16,5]{2,4,3,1,0:T(8,128)} %fusion.23, ...), kind=kOutput, calls=%fused_computation.7 | convolution fusion | flops 67502080 | bytes 19701960 | tf_op jit(solution)/shard_map/rvw,rwatn->rvatn/dot_general | solution.py:81
  565.8 11.6 %copy.254 = f32[2,5,16,256,16]{4,3,2,1,0:T(8,128)} copy(f32[2,5,16,256,16]{3,1,4,2,0:T(8,128)} %fusion.6) | data formatting | bytes 5242880 | tf_op jit(solution)/shard_map/add | solution.py:150
  577.4 15.0 %reshape.375 = f32[2,5,16,1,4096]{4,3,2,1,0:T(1,128)} reshape(f32[2,5,16,256,16]{4,3,2,1,0:T(8,128)} %copy.254) | data formatting | bytes 5242880 | tf_op jit(solution)/shard_map/reshape | solution.py:151
  (243 shorter events, 82.7 us)
Async XLA Ops:
  0.0 134.3 %copy-start = (f32[2,5,5]{2,0,1:T(2,128)S(1)}, f32[2,5,5]{2,0,1:T(2,128)}, u32[]{:S(2)}) copy-start(f32[2,5,5]{2,0,1:T(2,128)} %param.11) | copy-start | bytes 604
  19.7 13.5 %copy-start.30 = (s32[2,256]{1,0:T(2,128)S(1)}, s32[2,256]{1,0:T(2,128)}, u32[]{:S(2)}) copy-start(s32[2,256]{1,0:T(2,128)} %param.14) | copy-start | bytes 6148
  19.7 13.5 %copy-start.22 = (s32[4]{0:T(128)S(1)}, s32[4]{0:T(128)}, u32[]{:S(2)}) copy-start(s32[4]{0:T(128)} %param.17) | copy-start | bytes 52
  19.7 14.1 %copy-start.31 = (s32[2,256]{1,0:T(2,128)S(1)}, s32[2,256]{1,0:T(2,128)}, u32[]{:S(2)}) copy-start(s32[2,256]{1,0:T(2,128)} %param.15) | copy-start | bytes 6148
  19.7 14.1 %copy-start.32 = (s32[2]{0:T(128)S(1)}, s32[2]{0:T(128)}, u32[]{:S(2)}) copy-start(s32[2]{0:T(128)} %param.16) | copy-start | bytes 28
  23.5 35.0 %all-to-all-start = ((f32[16,2,5,256,8]{3,4,2,1,0:T(8,128)}), f32[16,2,5,256,8]{3,4,2,1,0:T(8,128)S(1)}, u32[]{:S(2)}, u32[]{:S(2)}) async-start(f32[16,2,5,256,8]{3,4,2,1,0:T(8,128)} %copy_dynamic-update-slice_fusion.4), calls=%async_computation | async-start | bytes 2621440 | tf_op jit(solution)/shard_map/all_to_all | solution.py:125
  50.2 11.4 %copy-start.19 = (f32[2,5,5]{2,0,1:T(2,128)S(1)}, f32[2,5,5]{2,0,1:T(2,128)}, u32[]{:S(2)}) copy-start(f32[2,5,5]{2,0,1:T(2,128)} %param.12) | copy-start | bytes 604
  58.6 3.3 copy-start.7
  58.6 6.7 %copy-start.20 = (f32[2,5,5]{2,0,1:T(2,128)S(1)}, f32[2,5,5]{2,0,1:T(2,128)}, u32[]{:S(2)}) copy-start(f32[2,5,5]{2,0,1:T(2,128)} %param.13) | copy-start | bytes 604
  68.0 58.6 %all-to-all-start.1 = ((f32[16,2,5,256,8]{3,4,2,1,0:T(8,128)}), f32[16,2,5,256,8]{3,4,2,1,0:T(8,128)S(1)}, u32[]{:S(2)}, u32[]{:S(2)}) async-start(f32[16,2,5,256,8]{3,4,2,1,0:T(8,128)} %pad_maximum_fusion.37), calls=%async_computation.1 | async-start | bytes 2621440 | tf_op jit(solution)/shard_map/all_to_all | solution.py:134
  90.8 35.9 %copy-start.21 = (f32[2,5,5]{2,0,1:T(2,128)S(1)}, f32[2,5,5]{2,0,1:T(2,128)}, u32[]{:S(2)}) copy-start(f32[2,5,5]{2,0,1:T(2,128)} %param.10) | copy-start | bytes 604
  92.7 30.5 %collective-permute-start.2 = (f32[2,5,16,256,1]{3,1,4,2,0:T(8,128)}, f32[2,5,16,256,1]{3,1,4,2,0:T(8,128)}, u32[]{:S(2)}, u32[]{:S(2)}) collective-permute-start(f32[2,5,16,256,1]{3,1,4,2,0:T(8,128)} %get-tuple-element.43), channel_id=1, source_target_pairs={{1,0},{2,1},{3,2},{4,3},{5,4},{6,5},{7,6},{8,7},{9,8},{10,9},{11,1... | collective-permute-start | bytes 491528 | tf_op jit(solution)/shard_map/ppermute | solution.py:34
  99.3 18.4 %collective-permute-start = (f32[2,5,16,1,16]{4,2,3,1,0:T(8,128)}, f32[2,5,16,1,16]{4,2,3,1,0:T(8,128)}, u32[]{:S(2)}, u32[]{:S(2)}) collective-permute-start(f32[2,5,16,1,16]{4,2,3,1,0:T(8,128)} %bitcast.34), channel_id=1, source_target_pairs={{8,0},{9,1},{10,2},{11,3},{12,4},{13,5},{14,6},{15,7},{0,8},{1,9},... | collective-permute-start | bytes 30728 | tf_op jit(solution)/shard_map/ppermute | solution.py:23
  99.3 21.6 %collective-permute-start.1 = (f32[2,5,16,1,16]{4,2,3,1,0:T(8,128)}, f32[2,5,16,1,16]{4,2,3,1,0:T(8,128)S(1)}, u32[]{:S(2)}, u32[]{:S(2)}) collective-permute-start(f32[2,5,16,1,16]{4,2,3,1,0:T(8,128)} %bitcast.35), channel_id=1, source_target_pairs={{8,0},{9,1},{10,2},{11,3},{12,4},{13,5},{14,6},{15,7},{0,8},{1,9},... | collective-permute-start | bytes 30728 | tf_op jit(solution)/shard_map/ppermute | solution.py:23
  102.2 22.7 %collective-permute-start.3 = (f32[2,5,16,256,1]{3,1,4,2,0:T(8,128)}, f32[2,5,16,256,1]{3,1,4,2,0:T(8,128)}, u32[]{:S(2)}, u32[]{:S(2)}) collective-permute-start(f32[2,5,16,256,1]{3,1,4,2,0:T(8,128)} %get-tuple-element.44), channel_id=1, source_target_pairs={{0,1},{1,2},{2,3},{3,4},{4,5},{5,6},{6,7},{7,8},{8,9},{9,10},{10,1... | collective-permute-start | bytes 491528 | tf_op jit(solution)/shard_map/ppermute | solution.py:33
  126.7 7.6 %copy-start.13 = (f32[2,5,1,256,16]{3,1,4,2,0:T(8,128)}, f32[2,5,1,256,16]{3,1,4,2,0:T(8,128)S(1)}, u32[]{:S(2)}) copy-start(f32[2,5,1,256,16]{3,1,4,2,0:T(8,128)S(1)} %pad_bitcast_fusion.6) | copy-start | bytes 491524
  126.7 7.5 %copy-start.14 = (f32[2,5,1,256,16]{3,1,4,2,0:T(8,128)}, f32[2,5,1,256,16]{3,1,4,2,0:T(8,128)S(1)}, u32[]{:S(2)}) copy-start(f32[2,5,1,256,16]{3,1,4,2,0:T(8,128)S(1)} %pad_bitcast_fusion.7) | copy-start | bytes 491524
  126.8 7.5 %copy-start.5 = (f32[2,5,16,256,16]{3,1,4,2,0:T(8,128)S(1)}, f32[2,5,16,256,16]{3,1,4,2,0:T(8,128)}, u32[]{:S(2)}) copy-start(f32[2,5,16,256,16]{3,1,4,2,0:T(8,128)} %copy.253) | copy-start | bytes 7864324
  126.8 7.5 %copy-start.11 = (f32[2,5,16,1,16]{3,1,4,2,0:T(8,128)S(1)}, f32[2,5,16,1,16]{3,1,4,2,0:T(8,128)}, u32[]{:S(2)}) copy-start(f32[2,5,16,1,16]{3,1,4,2,0:T(8,128)} %copy.189) | copy-start | bytes 30724
  126.8 7.5 %copy-start.12 = (f32[2,5,16,1,16]{3,1,4,2,0:T(8,128)S(1)}, f32[2,5,16,1,16]{3,1,4,2,0:T(8,128)}, u32[]{:S(2)}) copy-start(f32[2,5,16,1,16]{3,1,4,2,0:T(8,128)} %copy.191) | copy-start | bytes 30724
  126.8 7.5 %copy-start.15 = (f32[2,5,16,256,1]{3,1,4,2,0:T(8,128)S(1)}, f32[2,5,16,256,1]{3,1,4,2,0:T(8,128)}, u32[]{:S(2)}) copy-start(f32[2,5,16,256,1]{3,1,4,2,0:T(8,128)} %broadcast_multiply_fusion.7) | copy-start | bytes 491524
  126.8 7.5 %copy-start.16 = (f32[2,5,16,256,1]{3,1,4,2,0:T(8,128)S(1)}, f32[2,5,16,256,1]{3,1,4,2,0:T(8,128)}, u32[]{:S(2)}) copy-start(f32[2,5,16,256,1]{3,1,4,2,0:T(8,128)} %broadcast_multiply_fusion.3) | copy-start | bytes 491524
  146.3 2.0 copy-start.4
  146.3 7.9 %copy-start.33 = (f32[256]{0:T(256)S(1)}, f32[256]{0:T(256)}, u32[]{:S(2)}) copy-start(f32[256]{0:T(256)} %get-tuple-element.104) | copy-start | bytes 3076
  146.3 8.4 %copy-start.23 = (f32[256]{0:T(256)S(1)}, f32[256]{0:T(256)}, u32[]{:S(2)}) copy-start(f32[256]{0:T(256)} %get-tuple-element.59) | copy-start | bytes 3076
  146.3 10.1 %copy-start.27 = (f32[256]{0:T(256)S(1)}, f32[256]{0:T(256)}, u32[]{:S(2)}) copy-start(f32[256]{0:T(256)} %get-tuple-element.66) | copy-start | bytes 3076
  146.3 11.3 %copy-start.24 = (f32[256]{0:T(256)S(1)}, f32[256]{0:T(256)}, u32[]{:S(2)}) copy-start(f32[256]{0:T(256)} %get-tuple-element.65) | copy-start | bytes 3076
  150.3 31.2 %all-to-all-start.2 = ((f32[16,2,5,256,8]{3,4,2,1,0:T(8,128)}), f32[16,2,5,256,8]{3,4,2,1,0:T(8,128)S(1)}, u32[]{:S(2)}, u32[]{:S(2)}) async-start(f32[16,2,5,256,8]{3,4,2,1,0:T(8,128)} %fusion.128), calls=%async_computation.2 | async-start | bytes 2621440 | tf_op jit(solution)/shard_map/all_to_all | solution.py:125
  181.6 3.3 copy-start.9
  191.0 68.1 %all-to-all-start.3 = ((f32[16,2,5,256,8]{3,4,2,1,0:T(8,128)}), f32[16,2,5,256,8]{3,4,2,1,0:T(8,128)S(1)}, u32[]{:S(2)}, u32[]{:S(2)}) async-start(f32[16,2,5,256,8]{3,4,2,1,0:T(8,128)} %pad_maximum_fusion.39), calls=%async_computation.3 | async-start | bytes 2621440 | tf_op jit(solution)/shard_map/all_to_all | solution.py:134
  206.5 30.6 %collective-permute-start.4 = (f32[2,5,16,1,16]{4,2,3,1,0:T(8,128)S(1)}, f32[2,5,16,1,16]{4,2,3,1,0:T(8,128)}, u32[]{:S(2)}, u32[]{:S(2)}) collective-permute-start(f32[2,5,16,1,16]{4,2,3,1,0:T(8,128)S(1)} %copy.212), channel_id=1, source_target_pairs={{8,0},{9,1},{10,2},{11,3},{12,4},{13,5},{14,6},{15,7},{0,8},{1,9},... | collective-permute-start | bytes 30728 | tf_op jit(solution)/shard_map/ppermute | solution.py:23
  212.6 27.7 %collective-permute-start.5 = (f32[2,5,16,1,16]{4,2,3,1,0:T(8,128)}, f32[2,5,16,1,16]{4,2,3,1,0:T(8,128)}, u32[]{:S(2)}, u32[]{:S(2)}) collective-permute-start(f32[2,5,16,1,16]{4,2,3,1,0:T(8,128)} %copy.214), channel_id=1, source_target_pairs={{8,0},{9,1},{10,2},{11,3},{12,4},{13,5},{14,6},{15,7},{0,8},{1,9},... | collective-permute-start | bytes 30728 | tf_op jit(solution)/shard_map/ppermute | solution.py:23
  214.6 41.3 %collective-permute-start.6 = (f32[2,5,16,256,1]{3,1,4,2,0:T(8,128)}, f32[2,5,16,256,1]{3,1,4,2,0:T(8,128)}, u32[]{:S(2)}, u32[]{:S(2)}) collective-permute-start(f32[2,5,16,256,1]{3,1,4,2,0:T(8,128)} %get-tuple-element.41), channel_id=1, source_target_pairs={{1,0},{2,1},{3,2},{4,3},{5,4},{6,5},{7,6},{8,7},{9,8},{10,9},{11,1... | collective-permute-start | bytes 491528 | tf_op jit(solution)/shard_map/ppermute | solution.py:34
  218.4 39.1 %collective-permute-start.7 = (f32[2,5,16,256,1]{3,1,4,2,0:T(8,128)}, f32[2,5,16,256,1]{3,1,4,2,0:T(8,128)}, u32[]{:S(2)}, u32[]{:S(2)}) collective-permute-start(f32[2,5,16,256,1]{3,1,4,2,0:T(8,128)} %get-tuple-element.42), channel_id=1, source_target_pairs={{0,1},{1,2},{2,3},{3,4},{4,5},{5,6},{6,7},{7,8},{8,9},{9,10},{10,1... | collective-permute-start | bytes 491528 | tf_op jit(solution)/shard_map/ppermute | solution.py:33
  286.4 2.0 copy-start.1
  286.4 10.1 %copy-start.28 = (f32[256]{0:T(256)S(1)}, f32[256]{0:T(256)}, u32[]{:S(2)}) copy-start(f32[256]{0:T(256)} %get-tuple-element.6) | copy-start | bytes 3076
  286.4 10.1 %copy-start.29 = (f32[256]{0:T(256)S(1)}, f32[256]{0:T(256)}, u32[]{:S(2)}) copy-start(f32[256]{0:T(256)} %get-tuple-element.58) | copy-start | bytes 3076
  286.4 13.5 %copy-start.26 = (f32[256]{0:T(256)S(1)}, f32[256]{0:T(256)}, u32[]{:S(2)}) copy-start(f32[256]{0:T(256)} %get-tuple-element.64) | copy-start | bytes 3076
  290.4 33.5 %all-to-all-start.4 = ((f32[16,2,5,256,8]{3,4,2,1,0:T(8,128)}), f32[16,2,5,256,8]{3,4,2,1,0:T(8,128)S(1)}, u32[]{:S(2)}, u32[]{:S(2)}) async-start(f32[16,2,5,256,8]{3,4,2,1,0:T(8,128)} %fusion.129), calls=%async_computation.4 | async-start | bytes 2621440 | tf_op jit(solution)/shard_map/all_to_all | solution.py:125
  324.0 3.3 copy-start.10
  333.5 59.1 %all-to-all-start.5 = ((f32[16,2,5,256,8]{3,4,2,1,0:T(8,128)}), f32[16,2,5,256,8]{3,4,2,1,0:T(8,128)S(1)}, u32[]{:S(2)}, u32[]{:S(2)}) async-start(f32[16,2,5,256,8]{3,4,2,1,0:T(8,128)} %pad_maximum_fusion.41), calls=%async_computation.5 | async-start | bytes 2621440 | tf_op jit(solution)/shard_map/all_to_all | solution.py:134
  343.3 45.8 %collective-permute-start.10 = (f32[2,5,16,256,1]{3,1,4,2,0:T(8,128)}, f32[2,5,16,256,1]{3,1,4,2,0:T(8,128)}, u32[]{:S(2)}, u32[]{:S(2)}) collective-permute-start(f32[2,5,16,256,1]{3,1,4,2,0:T(8,128)} %get-tuple-element.35), channel_id=1, source_target_pairs={{1,0},{2,1},{3,2},{4,3},{5,4},{6,5},{7,6},{8,7},{9,8},{10,9},{11,1... | collective-permute-start | bytes 491528 | tf_op jit(solution)/shard_map/ppermute | solution.py:34
  355.2 27.5 %collective-permute-start.8 = (f32[2,5,16,1,16]{4,2,3,1,0:T(8,128)S(1)}, f32[2,5,16,1,16]{4,2,3,1,0:T(8,128)}, u32[]{:S(2)}, u32[]{:S(2)}) collective-permute-start(f32[2,5,16,1,16]{4,2,3,1,0:T(8,128)S(1)} %copy.230), channel_id=1, source_target_pairs={{8,0},{9,1},{10,2},{11,3},{12,4},{13,5},{14,6},{15,7},{0,8},{1,9},... | collective-permute-start | bytes 30728 | tf_op jit(solution)/shard_map/ppermute | solution.py:23
  358.5 27.5 %collective-permute-start.9 = (f32[2,5,16,1,16]{4,2,3,1,0:T(8,128)}, f32[2,5,16,1,16]{4,2,3,1,0:T(8,128)}, u32[]{:S(2)}, u32[]{:S(2)}) collective-permute-start(f32[2,5,16,1,16]{4,2,3,1,0:T(8,128)} %copy.232), channel_id=1, source_target_pairs={{8,0},{9,1},{10,2},{11,3},{12,4},{13,5},{14,6},{15,7},{0,8},{1,9},... | collective-permute-start | bytes 30728 | tf_op jit(solution)/shard_map/ppermute | solution.py:23
  361.4 29.5 %collective-permute-start.11 = (f32[2,5,16,256,1]{3,1,4,2,0:T(8,128)}, f32[2,5,16,256,1]{3,1,4,2,0:T(8,128)}, u32[]{:S(2)}, u32[]{:S(2)}) collective-permute-start(f32[2,5,16,256,1]{3,1,4,2,0:T(8,128)} %get-tuple-element.36), channel_id=1, source_target_pairs={{0,1},{1,2},{2,3},{3,4},{4,5},{5,6},{6,7},{7,8},{8,9},{9,10},{10,1... | collective-permute-start | bytes 491528 | tf_op jit(solution)/shard_map/ppermute | solution.py:33
  392.7 7.5 %copy-start.2 = (f32[2,5,16,256,16]{3,1,4,2,0:T(8,128)S(1)}, f32[2,5,16,256,16]{3,1,4,2,0:T(8,128)}, u32[]{:S(2)}) copy-start(f32[2,5,16,256,16]{3,1,4,2,0:T(8,128)} %copy-done.1) | copy-start | bytes 7864324
  392.7 7.5 %copy-start.6 = (f32[2,5,16,256,16]{3,1,4,2,0:T(8,128)S(1)}, f32[2,5,16,256,16]{3,1,4,2,0:T(8,128)}, u32[]{:S(2)}) copy-start(f32[2,5,16,256,16]{3,1,4,2,0:T(8,128)} %copy.253) | copy-start | bytes 7864324
  392.7 7.5 %copy-start.17 = (f32[2,5,16,256,1]{3,1,4,2,0:T(8,128)S(1)}, f32[2,5,16,256,1]{3,1,4,2,0:T(8,128)}, u32[]{:S(2)}) copy-start(f32[2,5,16,256,1]{3,1,4,2,0:T(8,128)} %broadcast_multiply_fusion.5) | copy-start | bytes 491524
  392.7 7.5 %copy-start.18 = (f32[2,5,16,256,1]{3,1,4,2,0:T(8,128)S(1)}, f32[2,5,16,256,1]{3,1,4,2,0:T(8,128)}, u32[]{:S(2)}) copy-start(f32[2,5,16,256,1]{3,1,4,2,0:T(8,128)} %broadcast_multiply_fusion.1) | copy-start | bytes 491524
  415.1 2.1 copy-start.3
  415.1 8.0 %copy-start.34 = (f32[256]{0:T(256)S(1)}, f32[256]{0:T(256)}, u32[]{:S(2)}) copy-start(f32[256]{0:T(256)} %get-tuple-element.102) | copy-start | bytes 3076
  415.1 10.2 %copy-start.25 = (f32[256]{0:T(256)S(1)}, f32[256]{0:T(256)}, u32[]{:S(2)}) copy-start(f32[256]{0:T(256)} %get-tuple-element.8) | copy-start | bytes 3076
  419.1 31.3 %all-to-all-start.6 = ((f32[16,2,5,256,8]{3,4,2,1,0:T(8,128)}), f32[16,2,5,256,8]{3,4,2,1,0:T(8,128)S(1)}, u32[]{:S(2)}, u32[]{:S(2)}) async-start(f32[16,2,5,256,8]{3,4,2,1,0:T(8,128)} %fusion.130), calls=%async_computation.6 | async-start | bytes 2621440 | tf_op jit(solution)/shard_map/all_to_all | solution.py:125
  450.5 3.3 copy-start.8
  459.8 66.5 %all-to-all-start.7 = ((f32[16,2,5,256,8]{3,4,2,1,0:T(8,128)}), f32[16,2,5,256,8]{3,4,2,1,0:T(8,128)S(1)}, u32[]{:S(2)}, u32[]{:S(2)}) async-start(f32[16,2,5,256,8]{3,4,2,1,0:T(8,128)} %pad_maximum_fusion.43), calls=%async_computation.7 | async-start | bytes 2621440 | tf_op jit(solution)/shard_map/all_to_all | solution.py:134
  474.7 31.1 %collective-permute-start.12 = (f32[2,5,16,1,16]{4,2,3,1,0:T(8,128)S(1)}, f32[2,5,16,1,16]{4,2,3,1,0:T(8,128)}, u32[]{:S(2)}, u32[]{:S(2)}) collective-permute-start(f32[2,5,16,1,16]{4,2,3,1,0:T(8,128)S(1)} %copy.248), channel_id=1, source_target_pairs={{8,0},{9,1},{10,2},{11,3},{12,4},{13,5},{14,6},{15,7},{0,8},{1,9},... | collective-permute-start | bytes 30728 | tf_op jit(solution)/shard_map/ppermute | solution.py:23
  479.2 28.5 %collective-permute-start.13 = (f32[2,5,16,1,16]{4,2,3,1,0:T(8,128)}, f32[2,5,16,1,16]{4,2,3,1,0:T(8,128)}, u32[]{:S(2)}, u32[]{:S(2)}) collective-permute-start(f32[2,5,16,1,16]{4,2,3,1,0:T(8,128)} %copy.250), channel_id=1, source_target_pairs={{8,0},{9,1},{10,2},{11,3},{12,4},{13,5},{14,6},{15,7},{0,8},{1,9},... | collective-permute-start | bytes 30728 | tf_op jit(solution)/shard_map/ppermute | solution.py:23
  481.2 41.7 %collective-permute-start.14 = (f32[2,5,16,256,1]{3,1,4,2,0:T(8,128)}, f32[2,5,16,256,1]{3,1,4,2,0:T(8,128)}, u32[]{:S(2)}, u32[]{:S(2)}) collective-permute-start(f32[2,5,16,256,1]{3,1,4,2,0:T(8,128)} %get-tuple-element.29), channel_id=1, source_target_pairs={{1,0},{2,1},{3,2},{4,3},{5,4},{6,5},{7,6},{8,7},{9,8},{10,9},{11,1... | collective-permute-start | bytes 491528 | tf_op jit(solution)/shard_map/ppermute | solution.py:34
  485.0 39.6 %collective-permute-start.15 = (f32[2,5,16,256,1]{3,1,4,2,0:T(8,128)}, f32[2,5,16,256,1]{3,1,4,2,0:T(8,128)}, u32[]{:S(2)}, u32[]{:S(2)}) collective-permute-start(f32[2,5,16,256,1]{3,1,4,2,0:T(8,128)} %get-tuple-element.30), channel_id=1, source_target_pairs={{0,1},{1,2},{2,3},{3,4},{4,5},{5,6},{6,7},{7,8},{8,9},{9,10},{10,1... | collective-permute-start | bytes 491528 | tf_op jit(solution)/shard_map/ppermute | solution.py:33
where the time goes:
time: 603 us; the launch traced here: 593 us
  matrix products  164 us (27%)
  waiting for transfers between devices  150 us (25%)
  local copies, waits for them, and re-layouts  139 us (23%)
  starting transfers between devices  82.8 us (14%)
  other arithmetic  54.9 us (9%)
    dot_general x4, matrix products, stencil(): flux = jnp.einsum('rvw,rwatn->rvatn', axial_jac, d_axial, precision=precise)  81.3 us
    ppermute x8, waiting for transfers between devices, passed_along(): return lax.ppermute(block, axis, route)  75.7 us
    all_to_all x4, waiting for transfers between devices, rates(): lax.all_to_all(buffer, 'sector', split_axis=0, concat_axis=0, tiled=True)  74.2 us
    dot_general x4, matrix products, stencil(): jnp.einsum('rvw,rwatn->rvatn', circ_jac, d_circ, precision=precise)  51 us
    all_to_all x4, starting transfers between devices, rates(): lax.all_to_all(back, 'sector', split_axis=0, concat_axis=0, tiled=True)  32.4 us
    reshape x2, local copies, waits for them, and re-layouts, on_device(): grid = field.reshape(2, VARS, depth, slots, rows)  25.6 us
    ppermute x8, local copies, waits for them, and re-layouts, passed_along(): return lax.ppermute(block, axis, route)  23.5 us
    slice x6, local copies, waits for them, and re-layouts, rates(): before = passed_along(state[:, :, :, -1:], 'sector', NB)  22.2 us
  transfers between devices with their start and end apart: 24, of which 8 were waited for; matrix products, arithmetic and copies ran while one was open for 25% of the time, Pallas kernels for 0%

commit v1 on v0

--- a/solution.py
+++ b/solution.py
@@ -1,8 +1,12 @@
+import functools
 import math
 
 import jax
 import jax.numpy as jnp
+import numpy as np
 from jax import lax
+from jax.experimental import pallas as pl
+from jax.experimental.pallas import tpu as pltpu
 from jax.sharding import PartitionSpec as P
 
 NTH = 512
@@ -83,7 +87,7 @@
     return -flux + diffusion * (neighbours - 6.0 * state)
 
 
-def on_device(
+def general_path(
     field,
     axial_jac,
     circ_jac,
@@ -151,6 +155,349 @@
     return result.reshape(field.shape)
 
 
+ROWS = 32
+LANES = 128
+RADIAL = 16
+PER_ROW = LANES // RADIAL
+HALF = ROWS * PER_ROW
+STATE_STEP = (0.5 * time_step, 0.5 * time_step, time_step)
+SUM_STEP = (time_step / 6.0, time_step / 3.0, time_step / 3.0, time_step / 6.0)
+
+
+def split(x):
+    high = x.astype(jnp.bfloat16)
+    return high, (x - high.astype(jnp.float32)).astype(jnp.bfloat16)
+
+
+def split_tables():
+    point = np.arange(2 * HALF).reshape(2, ROWS, PER_ROW).transpose(0, 2, 1).reshape(2, HALF)
+    modes = np.arange(K)
+    phase = 2.0 * np.pi * ((point[:, :, None] * modes) % NTH) / NTH
+    weights = np.where(modes == 0, 1.0 / NTH, 2.0 / NTH)
+    forward = np.concatenate([np.cos(phase), -np.sin(phase)], axis=2).transpose(0, 2, 1)
+    inverse = np.concatenate([weights * np.cos(phase), -weights * np.sin(phase)], axis=2)
+
+    def both(x):
+        high = x.astype(jnp.bfloat16)
+        low = (x - high.astype(np.float64)).astype(jnp.bfloat16)
+        return np.stack([high, low], axis=1)
+
+    return both(forward), both(inverse)
+
+
+def dot3(a_high, a_low, b):
+    b_high, b_low = split(b)
+    dot = functools.partial(jnp.dot, preferred_element_type=jnp.float32)
+    return dot(a_high, b_high) + (dot(a_high, b_low) + dot(a_low, b_high))
+
+
+def turned(x, shift, axis=1):
+    if isinstance(shift, int):
+        shift = shift % x.shape[axis]
+        return x if shift == 0 else pltpu.roll(x, shift, axis)
+    return pltpu.roll(x, lax.rem(shift + 2 * LANES, LANES), axis)
+
+
+def packed(planes):
+    group = lax.broadcasted_iota(jnp.int32, (ROWS, LANES), 1) // RADIAL
+    parts = []
+    for c in range(PER_ROW):
+        part = jnp.zeros((ROWS, LANES), jnp.float32)
+        for v in range(VARS):
+            part = jnp.where(group == v, turned(planes[v], RADIAL * (v - c)), part)
+        parts.append(part)
+    return jnp.concatenate(parts, axis=0)
+
+
+def unpacked(x, v):
+    group = lax.broadcasted_iota(jnp.int32, (ROWS, LANES), 1) // RADIAL
+    plane = turned(x[:ROWS], -RADIAL * v)
+    for c in range(1, PER_ROW):
+        piece = turned(x[c * ROWS:(c + 1) * ROWS], RADIAL * (c - v))
+        plane = jnp.where(group == c, piece, plane)
+    return plane
+
+
+def step_kernel(
+    field, axial_jac, circ_jac, left_char, right_char, count, offset,
+    source, target, forward, inverse, out,
+    state, seam_in, radial_out, radial_in, circ_out, circ_in,
+    gather, phases, ghost_map, spectrum,
+    seam_send, seam_recv, radial_send, radial_recv, circ_send, circ_recv,
+):
+    depth = field.shape[2]
+    devices = 2 * NB
+    me = lax.axis_index("sector")
+    position = lax.rem(me + NB // 2, devices)
+    sector = position // NB
+    band = lax.rem(position, NB)
+    right = lax.rem(me + 1, devices)
+    left = lax.rem(me + devices - 1, devices)
+    partner = lax.rem(me + NB, devices)
+    low_keep = (band > 0).astype(jnp.float32)
+    high_keep = (band < NB - 1).astype(jnp.float32)
+
+    barrier = pltpu.get_barrier_semaphore()
+    for other in (left, right, partner):
+        pl.semaphore_signal(
+            barrier, inc=1, device_id={"sector": other}, device_id_type=pl.DeviceIdType.MESH
+        )
+
+    lane = lax.broadcasted_iota(jnp.int32, (ROWS, LANES), 1)
+    row = lax.broadcasted_iota(jnp.int32, (ROWS, LANES), 0)
+    radial = lane % RADIAL
+    lane1 = lax.broadcasted_iota(jnp.int32, (1, LANES), 1)
+    group1 = lane1 // RADIAL
+
+    def pack(slot, r, a, new):
+        last = jnp.zeros((1, LANES), jnp.float32)
+        first = jnp.zeros((1, LANES), jnp.float32)
+        here = radial == a
+        for v in range(VARS):
+            n = new[v]
+            radial_out[slot, 0, r, v] = jnp.where(
+                here, turned(n, a - (RADIAL - 1)), radial_out[slot, 0, r, v]
+            )
+            radial_out[slot, 1, r, v] = jnp.where(here, turned(n, a), radial_out[slot, 1, r, v])
+            last = jnp.where(group1 == v, turned(n[ROWS - 1:], RADIAL * (v + 1)), last)
+            first = jnp.where(group1 == v, turned(n[:1], RADIAL * v), first)
+        circ_out[slot, 0, r, pl.ds(a, 1), :] = last
+        circ_out[slot, 1, r, pl.ds(a, 1), :] = first
+
+    def take_in(i, carry):
+        r, a = i // depth, lax.rem(i, depth)
+        new = [field[r, v, a] for v in range(VARS)]
+        for v in range(VARS):
+            state[0, r, v, a + 1] = new[v]
+        pack(0, r, a, new)
+        return carry
+
+    lax.fori_loop(0, 2 * depth, take_in, 0)
+    for slot in range(2):
+        for v in range(VARS):
+            state[slot, 0, v, 0] = jnp.zeros((ROWS, LANES), jnp.float32)
+            state[slot, 1, v, depth + 1] = jnp.zeros((ROWS, LANES), jnp.float32)
+
+    pl.semaphore_wait(barrier, 3)
+
+    def remote(src, dst, send, recv, device):
+        return pltpu.make_async_remote_copy(
+            src_ref=src, dst_ref=dst, send_sem=send, recv_sem=recv,
+            device_id={"sector": device}, device_id_type=pl.DeviceIdType.MESH,
+        )
+
+    def copies(k, cur):
+        seams = [
+            remote(
+                state.at[cur, d, :, depth if d == 0 else 1], seam_in.at[k, d],
+                seam_send.at[k, d], seam_recv.at[k, d], partner,
+            )
+            for d in range(2)
+        ]
+        sides = [
+            remote(
+                radial_out.at[k, d], radial_in.at[k, d],
+                radial_send.at[k, d], radial_recv.at[k, d], right if d == 0 else left,
+            )
+            for d in range(2)
+        ]
+        circ = remote(circ_out.at[k], circ_in.at[k], circ_send.at[k], circ_recv.at[k], partner)
+        return seams, sides, circ
+
+    def tables():
+        wide = lax.broadcasted_iota(jnp.int32, (K, K), 0)
+        pair = lax.broadcasted_iota(jnp.int32, (K, K), 1)
+        for d in range(2):
+            from_source = (source[d:d + 1, :] == wide).astype(jnp.float32).astype(jnp.bfloat16)
+            to_target = jnp.where(
+                (target[d:d + 1, :] == wide) & (pair < count[d]), 1.0, 0.0
+            ).astype(jnp.bfloat16)
+            moves = lax.dot_general(
+                to_target, from_source, (((1,), (1,)), ((), ())),
+                preferred_element_type=jnp.float32,
+            ).astype(jnp.bfloat16)
+            for part in range(2):
+                for wave in range(2):
+                    gather[d, part, :, wave * K:(wave + 1) * K] = jnp.dot(
+                        inverse[sector, part, :, wave * K:(wave + 1) * K], moves,
+                        preferred_element_type=jnp.float32,
+                    ).astype(jnp.bfloat16)
+            for v in range(VARS):
+                for w in range(VARS):
+                    total = right_char[d, v, 0] * left_char[d, 0, w]
+                    for c in range(1, VARS):
+                        total = total + right_char[d, v, c] * left_char[d, c, w]
+                    ghost_map[d, v * VARS + w] = total
+        mode = lax.broadcasted_iota(jnp.int32, (K, LANES), 0)
+        for s in range(4):
+            angle = ((mode * offset[s]) & (NTH - 1)).astype(jnp.float32) * (2.0 * math.pi / NTH)
+            phases[s, 0] = jnp.cos(angle)
+            phases[s, 1] = jnp.sin(angle)
+
+    def own_spectrum(cur):
+        both = jnp.concatenate(
+            [
+                packed([state[cur, 0, v, depth] for v in range(VARS)]),
+                packed([state[cur, 1, v, 1] for v in range(VARS)]),
+            ],
+            axis=1,
+        )
+        spectrum[...] = dot3(forward[sector, 0], forward[sector, 1], both)
+
+    def make_ghosts(k, cur):
+        both = jnp.concatenate(
+            [packed([seam_in[k, d, v] for v in range(VARS)]) for d in range(2)], axis=1
+        )
+        whole = spectrum[...] + dot3(forward[1 - sector, 0], forward[1 - sector, 1], both)
+        cosine, sine = phases[k, 0], phases[k, 1]
+        for d in range(2):
+            even = whole[:K, d * LANES:(d + 1) * LANES]
+            odd = whole[K:, d * LANES:(d + 1) * LANES]
+            turn = sine if d == 0 else -sine
+            moved = jnp.concatenate([cosine * even - turn * odd, turn * even + cosine * odd], axis=0)
+            raw = dot3(gather[d, 0], gather[d, 1], moved)
+            planes = [unpacked(raw, w) for w in range(VARS)]
+            for v in range(VARS):
+                ghost = ghost_map[d, v * VARS] * planes[0]
+                for w in range(1, VARS):
+                    ghost = ghost + ghost_map[d, v * VARS + w] * planes[w]
+                if d == 0:
+                    state[cur, 1, v, 0] = ghost
+                else:
+                    state[cur, 0, v, depth + 1] = ghost
+
+    def advance(k, cur, r, a, first, last):
+        up_row = circ_in[k, 0, r, pl.ds(a, 1), :]
+        down_row = circ_in[k, 1, r, pl.ds(a, 1), :]
+        along, around, spread = [], [], []
+        for w in range(VARS):
+            x = state[cur, r, w, a + 1]
+            before, after = state[cur, r, w, a], state[cur, r, w, a + 2]
+            up = jnp.where(row == 0, turned(up_row, LANES - RADIAL - RADIAL * w), turned(x, 1, 0))
+            down = jnp.where(row == ROWS - 1, turned(down_row, -RADIAL * w), turned(x, -1, 0))
+            previous = turned(jnp.where(lane >= LANES - RADIAL, up, x), RADIAL)
+            following = turned(jnp.where(lane < RADIAL, down, x), -RADIAL)
+            inner = jnp.where(
+                radial == 0, turned(radial_in[k, 0, r, w], -a) * low_keep, turned(x, 1)
+            )
+            outer = jnp.where(
+                radial == RADIAL - 1,
+                turned(radial_in[k, 1, r, w], RADIAL - 1 - a) * high_keep,
+                turned(x, -1),
+            )
+            along.append(after - before)
+            around.append(following - previous)
+            spread.append(
+                diffusion * ((after + before) + (following + previous) + (inner + outer) - 6.0 * x)
+            )
+        if last:
+            state_step, sum_step = None, SUM_STEP[3]
+        else:
+            state_step = jnp.where(k == 2, STATE_STEP[2], STATE_STEP[0])
+            sum_step = jnp.where(k == 0, SUM_STEP[0], SUM_STEP[1])
+        new = []
+        for v in range(VARS):
+            rate = spread[v]
+            for w in range(VARS):
+                rate = rate - (0.5 * axial_jac[r, v, w]) * along[w]
+                rate = rate - (0.5 * circ_jac[r, v, w]) * around[w]
+            if last:
+                out[r, v, a] = out[r, v, a] + sum_step * rate
+            else:
+                base = field[r, v, a]
+                total = jnp.where(k == 0, base, out[r, v, a])
+                out[r, v, a] = total + sum_step * rate
+                n = base + state_step * rate
+                state[1 - cur, r, v, a + 1] = n
+                new.append(n)
+        if not last:
+            pack(k + 1, r, a, new)
+
+    def stage(k, first=False, last=False):
+        cur = lax.rem(k, 2) if not isinstance(k, int) else k % 2
+        seams, sides, circ = copies(k, cur)
+        for copy in seams + sides + [circ]:
+            copy.start()
+        own_spectrum(cur)
+        for copy in sides + [circ]:
+            copy.wait_recv()
+
+        def inside(i, carry):
+            r = i // (depth - 1)
+            advance(k, cur, r, lax.rem(i, depth - 1) + r, first, last)
+            return carry
+
+        lax.fori_loop(0, 2 * (depth - 1), inside, 0)
+        for copy in seams:
+            copy.wait_recv()
+        make_ghosts(k, cur)
+
+        def edge(r, carry):
+            advance(k, cur, r, (depth - 1) * (1 - r), first, last)
+            return carry
+
+        lax.fori_loop(0, 2, edge, 0)
+        for copy in seams + sides + [circ]:
+            copy.wait_send()
+
+    tables()
+
+    def early(k, carry):
+        stage(k)
+        return carry
+
+    lax.fori_loop(0, 3, early, 0)
+    stage(3, last=True)
+
+
+def fast_path(
+    field, axial_jac, circ_jac, left_char, right_char, mode_source, mode_target, mode_count,
+    section_offset,
+):
+    depth = field.shape[2]
+    grid = field.reshape(2, VARS, depth, ROWS, LANES)
+    forward, inverse = split_tables()
+    smem = pl.BlockSpec(memory_space=pltpu.SMEM)
+    vmem = pl.BlockSpec(memory_space=pltpu.VMEM)
+    plane = (ROWS, LANES)
+    result = pl.pallas_call(
+        step_kernel,
+        out_shape=jax.ShapeDtypeStruct(grid.shape, jnp.float32),
+        in_specs=[vmem] + [smem] * 6 + [vmem] * 4,
+        out_specs=vmem,
+        scratch_shapes=[
+            pltpu.VMEM((2, 2, VARS, depth + 2) + plane, jnp.float32),
+            pltpu.VMEM((4, 2, VARS) + plane, jnp.float32),
+            pltpu.VMEM((4, 2, 2, VARS) + plane, jnp.float32),
+            pltpu.VMEM((4, 2, 2, VARS) + plane, jnp.float32),
+            pltpu.VMEM((4, 2, 2, depth, LANES), jnp.float32),
+            pltpu.VMEM((4, 2, 2, depth, LANES), jnp.float32),
+            pltpu.VMEM((2, 2, HALF, 2 * K), jnp.bfloat16),
+            pltpu.VMEM((4, 2, K, LANES), jnp.float32),
+            pltpu.SMEM((2, VARS * VARS), jnp.float32),
+            pltpu.VMEM((2 * K, 2 * LANES), jnp.float32),
+            pltpu.SemaphoreType.DMA((4, 2)),
+            pltpu.SemaphoreType.DMA((4, 2)),
+            pltpu.SemaphoreType.DMA((4, 2)),
+            pltpu.SemaphoreType.DMA((4, 2)),
+            pltpu.SemaphoreType.DMA((4,)),
+            pltpu.SemaphoreType.DMA((4,)),
+        ],
+        compiler_params=pltpu.CompilerParams(
+            collective_id=0, has_side_effects=True, vmem_limit_bytes=48 * 1024 * 1024
+        ),
+    )(
+        grid, axial_jac, circ_jac, left_char, right_char, mode_count, section_offset,
+        mode_source, mode_target, jnp.asarray(forward), jnp.asarray(inverse),
+    )
+    return result.reshape(field.shape)
+
+
+def on_device(field, *rest):
+    fits = lax.axis_size("sector") == 2 * NB and field.shape[4] == ROWS * LANES
+    return (fast_path if fits else general_path)(field, *rest)
+
+
 def solution(mesh):
     in_specs = (P("group", None, None, "sector", None), P(), P(), P(), P(), P(), P(), P(), P())
     out_specs = P("group", None, None, "sector", None)

time: 603 us -> 112 us (0.19); the launches traced: 593 us -> 111 us
  matrix products: 164 us -> 0 us
  waiting for transfers between devices: 150 us -> 0 us
  local copies, waits for them, and re-layouts: 139 us -> 9.38 us
  Pallas kernels: 0 us -> 102 us
  starting transfers between devices: 82.8 us -> 0 us
  other arithmetic: 54.9 us -> 0 us
    dot_general x44 -> x0, matrix products: 164 us -> none  [the longest x4 81.3 us: stencil(): flux = jnp.einsum('rvw,rwatn->rvatn', axial_jac, d_axial, precision=precise)]
    pallas_call x0 -> x1, Pallas kernels: none -> 102 us  [fast_path(): pl.pallas_call(step_kernel, out_shape=jax.ShapeDtypeStruct(grid.shape, jn...]
    ppermute x16 -> x0, waiting for transfers between devices: 75.8 us -> none  [the longest x8 75.7 us: passed_along(): return lax.ppermute(block, axis, route)]
    all_to_all x8 -> x0, waiting for transfers between devices: 74.2 us -> none  [the longest x4 74.2 us: rates(): lax.all_to_all(buffer, 'sector', split_axis=0, concat_axis=0, tiled=True)]
    all_to_all x8 -> x0, starting transfers between devices: 53.9 us -> none  [the longest x4 32.4 us: rates(): lax.all_to_all(back, 'sector', split_axis=0, concat_axis=0, tiled=True)]
    reshape x11 -> x0, local copies, waits for them, and re-layouts: 47.9 us -> none  [the longest x2 25.6 us: on_device(): grid = field.reshape(2, VARS, depth, slots, rows)]
    slice x52 -> x0, local copies, waits for them, and re-layouts: 43.7 us -> none  [the longest x6 22.2 us: rates(): before = passed_along(state[:, :, :, -1:], 'sector', NB)]
    ppermute x16 -> x0, starting transfers between devices: 28.9 us -> none  [the longest x4 16.5 us: with_halo(): after = lax.ppermute(first, axis, down)]
  transfers between devices with their start and end apart: 24 -> 0, of which waited for: 8 -> 0; matrix products, arithmetic and copies ran while one was open for 25% -> 0% of each run, Pallas kernels for 0% -> 0%
where the time goes in v1:
time: 112 us; the launch traced here: 111 us
  Pallas kernels  102 us (91%)
  local copies, waits for them, and re-layouts  9.38 us (8%)
    pallas_call x1, Pallas kernels, fast_path(): pl.pallas_call(step_kernel, out_shape=jax.ShapeDtypeStruct(grid.shape, jn...  102 us
    unnamed x17, local copies, waits for them, and re-layouts  9.38 us

profile of v1, /device:TPU:0, one launch (start us, length us, event | category | flops | bytes accessed | tf_op | source)
XLA Modules:
  0.0 111.1 jit_solution(1789863433011738241)
XLA Ops:
  0.0 0.7 copy.12.axial_jac
  0.7 0.7 copy.13.circ_jac
  1.4 0.7 copy.14.left_char
  2.1 0.7 copy.15.right_char
  2.8 0.0 copy-start
  2.8 1.2 %copy-done = bf16[2,2,256,512]{3,2,1,0:T(8,128)(2,1)S(1)} copy-done((bf16[2,2,256,512]{3,2,1,0:T(8,128)(2,1)S(1)}, bf16[2,2,256,512]{3,2,1,0:T(8,128)(2,1)}, u32[]{:S(2)}) %copy-start) | copy-done | bytes 1048600
  4.0 0.0 copy-start.1
  4.0 1.2 %copy-done.1 = bf16[2,2,512,256]{3,2,1,0:T(8,128)(2,1)S(1)} copy-done((bf16[2,2,512,256]{3,2,1,0:T(8,128)(2,1)S(1)}, bf16[2,2,512,256]{3,2,1,0:T(8,128)(2,1)}, u32[]{:S(2)}) %copy-start.1) | copy-done | bytes 1048600
  5.2 0.0 copy-start.2
  5.2 0.7 copy-done.2
  5.9 0.0 copy-start.3
  5.9 0.7 copy-done.3
  6.6 0.0 copy-start.4
  6.6 0.7 copy-done.4
  7.2 0.0 copy-start.5
  7.2 0.7 copy-done.5
  7.9 101.7 %shard_map.109 = f32[2,5,16,32,128]{4,3,2,1,0:T(8,128)S(1)} custom-call(f32[2,5,16,32,128]{4,3,2,1,0:T(8,128)} %bitcast.3, f32[2,5,5]{2,1,0:T(8,128)S(1)} %copy.12.axial_jac, f32[2,5,5]{2,1,0:T(8,128)S(1)} %copy.13.circ_jac, f32[2,5,5]{2,1,0:T(8,128)S(1)} %copy.14.left_char, f32[2,5,5]{2,1,0:T(8,128)S(1)} %copy.15.right_char, s32[2]{0:T(128)S(1)} %copy-done.4, ...), custom_call_target="tpu_custom_call" | custom-call | tf_op jit(solution)/shard_map/pallas_call | solution.py:463
  109.6 1.5 %copy.18 = f32[2,5,16,1,4096]{4,3,2,1,0:T(1,128)} copy(f32[2,5,16,1,4096]{4,3,2,1,0:T(1,128)S(1)} %bitcast.2) | data formatting | bytes 5242880
Async XLA Ops:
  2.8 1.2 %copy-start = (bf16[2,2,256,512]{3,2,1,0:T(8,128)(2,1)S(1)}, bf16[2,2,256,512]{3,2,1,0:T(8,128)(2,1)}, u32[]{:S(2)}) copy-start(bf16[2,2,256,512]{3,2,1,0:T(8,128)(2,1)} %constant.5.clone.inverse) | copy-start | bytes 3145732
  4.0 1.2 %copy-start.1 = (bf16[2,2,512,256]{3,2,1,0:T(8,128)(2,1)S(1)}, bf16[2,2,512,256]{3,2,1,0:T(8,128)(2,1)}, u32[]{:S(2)}) copy-start(bf16[2,2,512,256]{3,2,1,0:T(8,128)(2,1)} %constant.4.clone.forward) | copy-start | bytes 3145732
  5.2 0.7 copy-start.2
  5.9 0.7 copy-start.3
  6.6 0.7 copy-start.4
  7.2 0.7 copy-start.5

commit v2 on v1

--- a/solution.py
+++ b/solution.py
@@ -219,11 +219,15 @@
 
 
 def step_kernel(
+    field_hbm, axial_hbm, circ_hbm, left_hbm, right_hbm, count_hbm, offset_hbm,
+    source_hbm, target_hbm, forward_hbm, inverse_hbm, out,
     field, axial_jac, circ_jac, left_char, right_char, count, offset,
-    source, target, forward, inverse, out,
+    source, target, forward, inverse,
     state, seam_in, radial_out, radial_in, circ_out, circ_in,
-    gather, phases, ghost_map, spectrum,
-    seam_send, seam_recv, radial_send, radial_recv, circ_send, circ_recv,
+    rim_out, rim_in, corner_out, corner_in,
+    gather, phases, ghost_map, spectrum, factors,
+    load_sem, seam_send, seam_recv, radial_send, radial_recv, circ_send, circ_recv,
+    rim_send, rim_recv, corner_send, corner_recv,
 ):
     depth = field.shape[2]
     devices = 2 * NB
@@ -234,8 +238,17 @@
     right = lax.rem(me + 1, devices)
     left = lax.rem(me + devices - 1, devices)
     partner = lax.rem(me + NB, devices)
-    low_keep = (band > 0).astype(jnp.float32)
-    high_keep = (band < NB - 1).astype(jnp.float32)
+    has_left, has_right = band > 0, band < NB - 1
+
+    pairs = [(field_hbm.at[r], state.at[0, r, :, pl.ds(1, depth)]) for r in range(2)]
+    pairs += [
+        (field_hbm, field), (axial_hbm, axial_jac), (circ_hbm, circ_jac), (left_hbm, left_char),
+        (right_hbm, right_char), (count_hbm, count), (offset_hbm, offset), (source_hbm, source),
+        (target_hbm, target), (forward_hbm, forward), (inverse_hbm, inverse),
+    ]
+    loads = [pltpu.make_async_copy(a, b, load_sem.at[i]) for i, (a, b) in enumerate(pairs)]
+    for load in loads:
+        load.start()
 
     barrier = pltpu.get_barrier_semaphore()
     for other in (left, right, partner):
@@ -249,36 +262,42 @@
     lane1 = lax.broadcasted_iota(jnp.int32, (1, LANES), 1)
     group1 = lane1 // RADIAL
 
-    def pack(slot, r, a, new):
+    def edge_rows(new):
         last = jnp.zeros((1, LANES), jnp.float32)
         first = jnp.zeros((1, LANES), jnp.float32)
+        for v in range(VARS):
+            last = jnp.where(group1 == v, turned(new[v][ROWS - 1:], RADIAL * (v + 1)), last)
+            first = jnp.where(group1 == v, turned(new[v][:1], RADIAL * v), first)
+        return last, first
+
+    def pack(slot, r, a, new):
         here = radial == a
         for v in range(VARS):
-            n = new[v]
-            radial_out[slot, 0, r, v] = jnp.where(
-                here, turned(n, a - (RADIAL - 1)), radial_out[slot, 0, r, v]
+            radial_out[slot, r, 0, v] = jnp.where(
+                here, turned(new[v], a - (RADIAL - 1)), radial_out[slot, r, 0, v]
             )
-            radial_out[slot, 1, r, v] = jnp.where(here, turned(n, a), radial_out[slot, 1, r, v])
-            last = jnp.where(group1 == v, turned(n[ROWS - 1:], RADIAL * (v + 1)), last)
-            first = jnp.where(group1 == v, turned(n[:1], RADIAL * v), first)
-        circ_out[slot, 0, r, pl.ds(a, 1), :] = last
-        circ_out[slot, 1, r, pl.ds(a, 1), :] = first
-
-    def take_in(i, carry):
-        r, a = i // depth, lax.rem(i, depth)
-        new = [field[r, v, a] for v in range(VARS)]
-        for v in range(VARS):
-            state[0, r, v, a + 1] = new[v]
-        pack(0, r, a, new)
-        return carry
-
-    lax.fori_loop(0, 2 * depth, take_in, 0)
-    for slot in range(2):
-        for v in range(VARS):
-            state[slot, 0, v, 0] = jnp.zeros((ROWS, LANES), jnp.float32)
-            state[slot, 1, v, depth + 1] = jnp.zeros((ROWS, LANES), jnp.float32)
-
-    pl.semaphore_wait(barrier, 3)
+            radial_out[slot, r, 1, v] = jnp.where(
+                here, turned(new[v], a), radial_out[slot, r, 1, v]
+            )
+        last, first = edge_rows(new)
+        circ_out[slot, r, 0, pl.ds(a, 1), :] = last
+        circ_out[slot, r, 1, pl.ds(a, 1), :] = first
+
+    def pack_edges(slot, planes):
+        outer = jnp.zeros((ROWS, LANES), jnp.float32)
+        inner = jnp.zeros((ROWS, LANES), jnp.float32)
+        rows = []
+        for r in range(2):
+            for v in range(VARS):
+                place = r * VARS + v
+                outer = jnp.where(
+                    radial == place, turned(planes[r][v], place - (RADIAL - 1)), outer
+                )
+                inner = jnp.where(radial == place, turned(planes[r][v], place), inner)
+            rows += edge_rows(planes[r])
+        rim_out[slot, 0] = outer
+        rim_out[slot, 1] = inner
+        corner_out[slot] = jnp.concatenate(rows + [jnp.zeros((4, LANES), jnp.float32)], axis=0)
 
     def remote(src, dst, send, recv, device):
         return pltpu.make_async_remote_copy(
@@ -286,23 +305,57 @@
             device_id={"sector": device}, device_id_type=pl.DeviceIdType.MESH,
         )
 
-    def copies(k, cur):
-        seams = [
+    def seams(k, cur):
+        return [
             remote(
                 state.at[cur, d, :, depth if d == 0 else 1], seam_in.at[k, d],
                 seam_send.at[k, d], seam_recv.at[k, d], partner,
             )
             for d in range(2)
         ]
-        sides = [
+
+    def sides(k, r):
+        return [
             remote(
-                radial_out.at[k, d], radial_in.at[k, d],
-                radial_send.at[k, d], radial_recv.at[k, d], right if d == 0 else left,
+                radial_out.at[k, r, d], radial_in.at[k, r, d], radial_send.at[k, r, d],
+                radial_recv.at[k, r, d], right if d == 0 else left,
             )
             for d in range(2)
         ]
-        circ = remote(circ_out.at[k], circ_in.at[k], circ_send.at[k], circ_recv.at[k], partner)
-        return seams, sides, circ
+
+    def rims(k):
+        return [
+            remote(
+                rim_out.at[k, d], rim_in.at[k, d], rim_send.at[k, d], rim_recv.at[k, d],
+                right if d == 0 else left,
+            )
+            for d in range(2)
+        ]
+
+    def circs(k, r):
+        return remote(
+            circ_out.at[k, r], circ_in.at[k, r], circ_send.at[k, r], circ_recv.at[k, r], partner
+        )
+
+    def corners(k):
+        return remote(
+            corner_out.at[k], corner_in.at[k], corner_send.at[k], corner_recv.at[k], partner
+        )
+
+    def send(sideways, across):
+        for d, there in enumerate((has_right, has_left)):
+            pl.when(there)(sideways[d].start)
+        across.start()
+
+    def arrive(sideways, across):
+        for d, there in enumerate((has_left, has_right)):
+            pl.when(there)(sideways[d].wait_recv)
+        across.wait_recv()
+
+    def sent(sideways, across):
+        for d, there in enumerate((has_right, has_left)):
+            pl.when(there)(sideways[d].wait_send)
+        across.wait_send()
 
     def tables():
         wide = lax.broadcasted_iota(jnp.int32, (K, K), 0)
@@ -324,10 +377,12 @@
                     ).astype(jnp.bfloat16)
             for v in range(VARS):
                 for w in range(VARS):
-                    total = right_char[d, v, 0] * left_char[d, 0, w]
+                    total = right_char[v, d, 0] * left_char[0, d, w]
                     for c in range(1, VARS):
-                        total = total + right_char[d, v, c] * left_char[d, c, w]
+                        total = total + right_char[v, d, c] * left_char[c, d, w]
                     ghost_map[d, v * VARS + w] = total
+                    factors[0, d, v * VARS + w] = -0.5 * axial_jac[v, d, w]
+                    factors[1, d, v * VARS + w] = -0.5 * circ_jac[v, d, w]
         mode = lax.broadcasted_iota(jnp.int32, (K, LANES), 0)
         for s in range(4):
             angle = ((mode * offset[s]) & (NTH - 1)).astype(jnp.float32) * (2.0 * math.pi / NTH)
@@ -366,9 +421,13 @@
                 else:
                     state[cur, 0, v, depth + 1] = ghost
 
-    def advance(k, cur, r, a, first, last):
-        up_row = circ_in[k, 0, r, pl.ds(a, 1), :]
-        down_row = circ_in[k, 1, r, pl.ds(a, 1), :]
+    def advance(k, cur, r, a, last, edge):
+        if edge:
+            up_row = corner_in[k, 2 * r:2 * r + 1, :]
+            down_row = corner_in[k, 2 * r + 1:2 * r + 2, :]
+        else:
+            up_row = circ_in[k, r, 0, pl.ds(a, 1), :]
+            down_row = circ_in[k, r, 1, pl.ds(a, 1), :]
         along, around, spread = [], [], []
         for w in range(VARS):
             x = state[cur, r, w, a + 1]
@@ -377,21 +436,21 @@
             down = jnp.where(row == ROWS - 1, turned(down_row, -RADIAL * w), turned(x, -1, 0))
             previous = turned(jnp.where(lane >= LANES - RADIAL, up, x), RADIAL)
             following = turned(jnp.where(lane < RADIAL, down, x), -RADIAL)
-            inner = jnp.where(
-                radial == 0, turned(radial_in[k, 0, r, w], -a) * low_keep, turned(x, 1)
-            )
-            outer = jnp.where(
-                radial == RADIAL - 1,
-                turned(radial_in[k, 1, r, w], RADIAL - 1 - a) * high_keep,
-                turned(x, -1),
-            )
+            if edge:
+                place = r * VARS + w
+                low, high = turned(rim_in[k, 0], -place), turned(rim_in[k, 1], RADIAL - 1 - place)
+            else:
+                low = turned(radial_in[k, r, 0, w], -a)
+                high = turned(radial_in[k, r, 1, w], RADIAL - 1 - a)
+            inner = jnp.where(radial == 0, low, turned(x, 1))
+            outer = jnp.where(radial == RADIAL - 1, high, turned(x, -1))
             along.append(after - before)
             around.append(following - previous)
             spread.append(
                 diffusion * ((after + before) + (following + previous) + (inner + outer) - 6.0 * x)
             )
         if last:
-            state_step, sum_step = None, SUM_STEP[3]
+            sum_step = SUM_STEP[3]
         else:
             state_step = jnp.where(k == 2, STATE_STEP[2], STATE_STEP[0])
             sum_step = jnp.where(k == 0, SUM_STEP[0], SUM_STEP[1])
@@ -399,8 +458,8 @@
         for v in range(VARS):
             rate = spread[v]
             for w in range(VARS):
-                rate = rate - (0.5 * axial_jac[r, v, w]) * along[w]
-                rate = rate - (0.5 * circ_jac[r, v, w]) * around[w]
+                rate = rate + factors[0, r, v * VARS + w] * along[w]
+                rate = rate + factors[1, r, v * VARS + w] * around[w]
             if last:
                 out[r, v, a] = out[r, v, a] + sum_step * rate
             else:
@@ -410,37 +469,72 @@
                 n = base + state_step * rate
                 state[1 - cur, r, v, a + 1] = n
                 new.append(n)
-        if not last:
-            pack(k + 1, r, a, new)
-
-    def stage(k, first=False, last=False):
-        cur = lax.rem(k, 2) if not isinstance(k, int) else k % 2
-        seams, sides, circ = copies(k, cur)
-        for copy in seams + sides + [circ]:
-            copy.start()
-        own_spectrum(cur)
-        for copy in sides + [circ]:
-            copy.wait_recv()
-
-        def inside(i, carry):
-            r = i // (depth - 1)
-            advance(k, cur, r, lax.rem(i, depth - 1) + r, first, last)
-            return carry
-
-        lax.fori_loop(0, 2 * (depth - 1), inside, 0)
-        for copy in seams:
+        return new
+
+    def stage(k, last=False):
+        cur = k % 2 if isinstance(k, int) else lax.rem(k, 2)
+        for r in range(2):
+            arrive(sides(k, r), circs(k, r))
+
+            def inside(a, carry):
+                new = advance(k, cur, r, a, last, False)
+                if not last:
+                    pack(k + 1, r, a, new)
+                return carry
+
+            lax.fori_loop(r, depth - 1 + r, inside, 0)
+            if not last:
+                send(sides(k + 1, r), circs(k + 1, r))
+        for copy in seams(k, cur):
             copy.wait_recv()
         make_ghosts(k, cur)
-
-        def edge(r, carry):
-            advance(k, cur, r, (depth - 1) * (1 - r), first, last)
+        arrive(rims(k), corners(k))
+        planes = [advance(k, cur, r, (depth - 1) * (1 - r), last, True) for r in range(2)]
+        if not last:
+            for copy in seams(k + 1, 1 - cur):
+                copy.start()
+            pack_edges(k + 1, planes)
+            send(rims(k + 1), corners(k + 1))
+            own_spectrum(1 - cur)
+        for copy in seams(k, cur):
+            copy.wait_send()
+
+    for d, there in enumerate((has_left, has_right)):
+
+        @pl.when(jnp.logical_not(there))
+        def _():
+            for k in range(4):
+                rim_in[k, d] = jnp.zeros((ROWS, LANES), jnp.float32)
+                for r in range(2):
+                    radial_in[k, r, d] = jnp.zeros((VARS, ROWS, LANES), jnp.float32)
+
+    for slot in range(2):
+        for v in range(VARS):
+            state[slot, 0, v, 0] = jnp.zeros((ROWS, LANES), jnp.float32)
+            state[slot, 1, v, depth + 1] = jnp.zeros((ROWS, LANES), jnp.float32)
+
+    loads[0].wait()
+    loads[1].wait()
+    pl.semaphore_wait(barrier, 3)
+    for r in range(2):
+
+        def take_in(a, carry):
+            pack(0, r, a, [state[0, r, v, a + 1] for v in range(VARS)])
             return carry
 
-        lax.fori_loop(0, 2, edge, 0)
-        for copy in seams + sides + [circ]:
-            copy.wait_send()
-
+        lax.fori_loop(r, depth - 1 + r, take_in, 0)
+        send(sides(0, r), circs(0, r))
+        if r == 0:
+            for copy in seams(0, 0):
+                copy.start()
+    pack_edges(
+        0, [[state[0, 0, v, depth] for v in range(VARS)], [state[0, 1, v, 1] for v in range(VARS)]]
+    )
+    send(rims(0), corners(0))
+    for load in loads[2:]:
+        load.wait()
     tables()
+    own_spectrum(0)
 
     def early(k, carry):
         stage(k)
@@ -448,6 +542,10 @@
 
     lax.fori_loop(0, 3, early, 0)
     stage(3, last=True)
+    for k in range(4):
+        for r in range(2):
+            sent(sides(k, r), circs(k, r))
+        sent(rims(k), corners(k))
 
 
 def fast_path(
@@ -457,25 +555,39 @@
     depth = field.shape[2]
     grid = field.reshape(2, VARS, depth, ROWS, LANES)
     forward, inverse = split_tables()
-    smem = pl.BlockSpec(memory_space=pltpu.SMEM)
-    vmem = pl.BlockSpec(memory_space=pltpu.VMEM)
     plane = (ROWS, LANES)
+    small = [jnp.transpose(m, (1, 0, 2)) for m in (axial_jac, circ_jac, left_char, right_char)]
+    args = [
+        grid, *small, mode_count, section_offset, mode_source, mode_target,
+        jnp.asarray(forward), jnp.asarray(inverse),
+    ]
+    places = [pltpu.VMEM] + [pltpu.SMEM] * 6 + [pltpu.VMEM] * 4
     result = pl.pallas_call(
         step_kernel,
         out_shape=jax.ShapeDtypeStruct(grid.shape, jnp.float32),
-        in_specs=[vmem] + [smem] * 6 + [vmem] * 4,
-        out_specs=vmem,
-        scratch_shapes=[
+        in_specs=[pl.BlockSpec(memory_space=pltpu.HBM)] * len(args),
+        out_specs=pl.BlockSpec(memory_space=pltpu.VMEM),
+        scratch_shapes=[place(x.shape, x.dtype) for place, x in zip(places, args)] + [
             pltpu.VMEM((2, 2, VARS, depth + 2) + plane, jnp.float32),
             pltpu.VMEM((4, 2, VARS) + plane, jnp.float32),
             pltpu.VMEM((4, 2, 2, VARS) + plane, jnp.float32),
             pltpu.VMEM((4, 2, 2, VARS) + plane, jnp.float32),
             pltpu.VMEM((4, 2, 2, depth, LANES), jnp.float32),
             pltpu.VMEM((4, 2, 2, depth, LANES), jnp.float32),
+            pltpu.VMEM((4, 2) + plane, jnp.float32),
+            pltpu.VMEM((4, 2) + plane, jnp.float32),
+            pltpu.VMEM((4, 8, LANES), jnp.float32),
+            pltpu.VMEM((4, 8, LANES), jnp.float32),
             pltpu.VMEM((2, 2, HALF, 2 * K), jnp.bfloat16),
             pltpu.VMEM((4, 2, K, LANES), jnp.float32),
             pltpu.SMEM((2, VARS * VARS), jnp.float32),
             pltpu.VMEM((2 * K, 2 * LANES), jnp.float32),
+            pltpu.SMEM((2, 2, VARS * VARS), jnp.float32),
+            pltpu.SemaphoreType.DMA((len(args) + 2,)),
+            pltpu.SemaphoreType.DMA((4, 2)),
+            pltpu.SemaphoreType.DMA((4, 2)),
+            pltpu.SemaphoreType.DMA((4, 2, 2)),
+            pltpu.SemaphoreType.DMA((4, 2, 2)),
             pltpu.SemaphoreType.DMA((4, 2)),
             pltpu.SemaphoreType.DMA((4, 2)),
             pltpu.SemaphoreType.DMA((4, 2)),
@@ -484,12 +596,9 @@
             pltpu.SemaphoreType.DMA((4,)),
         ],
         compiler_params=pltpu.CompilerParams(
-            collective_id=0, has_side_effects=True, vmem_limit_bytes=48 * 1024 * 1024
+            collective_id=0, has_side_effects=True, vmem_limit_bytes=62 * 1024 * 1024
         ),
-    )(
-        grid, axial_jac, circ_jac, left_char, right_char, mode_count, section_offset,
-        mode_source, mode_target, jnp.asarray(forward), jnp.asarray(inverse),
-    )
+    )(*args)
     return result.reshape(field.shape)
 
 

time: 112 us -> 78.5 us (0.70)
  Pallas kernels: 102 us -> 72.9 us
  local copies, waits for them, and re-layouts: 9.38 us -> 5.4 us
    pallas_call x1, Pallas kernels: 102 us -> 72.9 us  [fast_path(): pl.pallas_call(step_kernel, out_shape=jax.ShapeDtypeStruct(grid.shape, jn...]
    unnamed x17 -> x1, local copies, waits for them, and re-layouts: 9.38 us -> 5.4 us
where the time goes in v2:
time: 78.5 us; the launch traced here: 78.3 us
  Pallas kernels  72.9 us (93%)
  local copies, waits for them, and re-layouts  5.4 us (7%)
    pallas_call x1, Pallas kernels, fast_path(): pl.pallas_call(step_kernel, out_shape=jax.ShapeDtypeStruct(grid.shape, jn...  72.9 us
    unnamed x1, local copies, waits for them, and re-layouts  5.4 us

profile of v2, /device:TPU:0, one launch (start us, length us, event | category | flops | bytes accessed | tf_op | source)
XLA Modules:
  0.0 78.3 jit_solution(18040587515321554381)
XLA Ops:
  0.0 72.9 %shard_map.109 = f32[2,5,16,32,128]{4,3,2,1,0:T(8,128)} custom-call(f32[2,5,16,32,128]{4,3,2,1,0:T(8,128)} %bitcast.7, f32[5,2,5]{2,1,0:T(2,128)} %bitcast.8, f32[5,2,5]{2,1,0:T(2,128)} %bitcast.9, f32[5,2,5]{2,1,0:T(2,128)} %bitcast.10, f32[5,2,5]{2,1,0:T(2,128)} %bitcast.11, s32[2]{0:T(128)} %count_hbm.1, s32[4]{0:T(128)} %offset_hbm.1, ...), custom_call_target="tpu_custom_call" | custom-call | tf_op jit(solution)/shard_map/pallas_call | solution.py:565
  72.9 5.4 %copy.14 = f32[2,5,16,1,4096]{4,3,2,1,0:T(1,128)} copy(f32[2,5,16,1,4096]{4,3,2,1,0:T(1,128)} %bitcast.6) | data formatting | bytes 5242880

commit v3 on v2

--- a/solution.py
+++ b/solution.py
@@ -161,7 +161,8 @@
 PER_ROW = LANES // RADIAL
 HALF = ROWS * PER_ROW
 STATE_STEP = (0.5 * time_step, 0.5 * time_step, time_step)
-SUM_STEP = (time_step / 6.0, time_step / 3.0, time_step / 3.0, time_step / 6.0)
+TILE = 8
+TOGETHER = 4
 
 
 def split(x):
@@ -221,7 +222,7 @@
 def step_kernel(
     field_hbm, axial_hbm, circ_hbm, left_hbm, right_hbm, count_hbm, offset_hbm,
     source_hbm, target_hbm, forward_hbm, inverse_hbm, out,
-    field, axial_jac, circ_jac, left_char, right_char, count, offset,
+    axial_jac, circ_jac, left_char, right_char, count, offset,
     source, target, forward, inverse,
     state, seam_in, radial_out, radial_in, circ_out, circ_in,
     rim_out, rim_in, corner_out, corner_in,
@@ -229,7 +230,7 @@
     load_sem, seam_send, seam_recv, radial_send, radial_recv, circ_send, circ_recv,
     rim_send, rim_recv, corner_send, corner_recv,
 ):
-    depth = field.shape[2]
+    depth = out.shape[2]
     devices = 2 * NB
     me = lax.axis_index("sector")
     position = lax.rem(me + NB // 2, devices)
@@ -242,7 +243,7 @@
 
     pairs = [(field_hbm.at[r], state.at[0, r, :, pl.ds(1, depth)]) for r in range(2)]
     pairs += [
-        (field_hbm, field), (axial_hbm, axial_jac), (circ_hbm, circ_jac), (left_hbm, left_char),
+        (axial_hbm, axial_jac), (circ_hbm, circ_jac), (left_hbm, left_char),
         (right_hbm, right_char), (count_hbm, count), (offset_hbm, offset), (source_hbm, source),
         (target_hbm, target), (forward_hbm, forward), (inverse_hbm, inverse),
     ]
@@ -262,13 +263,23 @@
     lane1 = lax.broadcasted_iota(jnp.int32, (1, LANES), 1)
     group1 = lane1 // RADIAL
 
-    def edge_rows(new):
+    row8 = lax.broadcasted_iota(jnp.int32, (TILE, LANES), 0)
+    lane8 = lax.broadcasted_iota(jnp.int32, (TILE, LANES), 1)
+    radial8 = lane8 % RADIAL
+    at_last, at_first = lane8 >= LANES - RADIAL, lane8 < RADIAL
+
+    def edge_rows(top, bottom):
         last = jnp.zeros((1, LANES), jnp.float32)
         first = jnp.zeros((1, LANES), jnp.float32)
         for v in range(VARS):
-            last = jnp.where(group1 == v, turned(new[v][ROWS - 1:], RADIAL * (v + 1)), last)
-            first = jnp.where(group1 == v, turned(new[v][:1], RADIAL * v), first)
+            last = jnp.where(group1 == v, turned(bottom[v], RADIAL * (v + 1)), last)
+            first = jnp.where(group1 == v, turned(top[v], RADIAL * v), first)
         return last, first
+
+    def pack_rows(slot, r, a, top, bottom):
+        last, first = edge_rows(top, bottom)
+        circ_out[slot, r, 0, pl.ds(a, 1), :] = last
+        circ_out[slot, r, 1, pl.ds(a, 1), :] = first
 
     def pack(slot, r, a, new):
         here = radial == a
@@ -279,22 +290,19 @@
             radial_out[slot, r, 1, v] = jnp.where(
                 here, turned(new[v], a), radial_out[slot, r, 1, v]
             )
-        last, first = edge_rows(new)
-        circ_out[slot, r, 0, pl.ds(a, 1), :] = last
-        circ_out[slot, r, 1, pl.ds(a, 1), :] = first
-
-    def pack_edges(slot, planes):
+        pack_rows(slot, r, a, [n[:1] for n in new], [n[ROWS - 1:] for n in new])
+
+    def pack_edges(slot):
         outer = jnp.zeros((ROWS, LANES), jnp.float32)
         inner = jnp.zeros((ROWS, LANES), jnp.float32)
         rows = []
         for r in range(2):
+            planes = [state[slot, r, v, depth if r == 0 else 1] for v in range(VARS)]
             for v in range(VARS):
                 place = r * VARS + v
-                outer = jnp.where(
-                    radial == place, turned(planes[r][v], place - (RADIAL - 1)), outer
-                )
-                inner = jnp.where(radial == place, turned(planes[r][v], place), inner)
-            rows += edge_rows(planes[r])
+                outer = jnp.where(radial == place, turned(planes[v], place - (RADIAL - 1)), outer)
+                inner = jnp.where(radial == place, turned(planes[v], place), inner)
+            rows += edge_rows([n[:1] for n in planes], [n[ROWS - 1:] for n in planes])
         rim_out[slot, 0] = outer
         rim_out[slot, 1] = inner
         corner_out[slot] = jnp.concatenate(rows + [jnp.zeros((4, LANES), jnp.float32)], axis=0)
@@ -305,10 +313,10 @@
             device_id={"sector": device}, device_id_type=pl.DeviceIdType.MESH,
         )
 
-    def seams(k, cur):
+    def seams(k):
         return [
             remote(
-                state.at[cur, d, :, depth if d == 0 else 1], seam_in.at[k, d],
+                state.at[k, d, :, depth if d == 0 else 1], seam_in.at[k, d],
                 seam_send.at[k, d], seam_recv.at[k, d], partner,
             )
             for d in range(2)
@@ -381,25 +389,27 @@
                     for c in range(1, VARS):
                         total = total + right_char[v, d, c] * left_char[c, d, w]
                     ghost_map[d, v * VARS + w] = total
-                    factors[0, d, v * VARS + w] = -0.5 * axial_jac[v, d, w]
-                    factors[1, d, v * VARS + w] = -0.5 * circ_jac[v, d, w]
+                    for which, jac in enumerate((axial_jac, circ_jac)):
+                        factors[which, d, v * VARS + w] = jnp.full(
+                            (TILE, LANES), (-0.5 / diffusion) * jac[v, d, w], jnp.float32
+                        )
         mode = lax.broadcasted_iota(jnp.int32, (K, LANES), 0)
         for s in range(4):
             angle = ((mode * offset[s]) & (NTH - 1)).astype(jnp.float32) * (2.0 * math.pi / NTH)
             phases[s, 0] = jnp.cos(angle)
             phases[s, 1] = jnp.sin(angle)
 
-    def own_spectrum(cur):
+    def own_spectrum(k):
         both = jnp.concatenate(
             [
-                packed([state[cur, 0, v, depth] for v in range(VARS)]),
-                packed([state[cur, 1, v, 1] for v in range(VARS)]),
+                packed([state[k, 0, v, depth] for v in range(VARS)]),
+                packed([state[k, 1, v, 1] for v in range(VARS)]),
             ],
             axis=1,
         )
         spectrum[...] = dot3(forward[sector, 0], forward[sector, 1], both)
 
-    def make_ghosts(k, cur):
+    def make_ghosts(k):
         both = jnp.concatenate(
             [packed([seam_in[k, d, v] for v in range(VARS)]) for d in range(2)], axis=1
         )
@@ -417,87 +427,109 @@
                 for w in range(1, VARS):
                     ghost = ghost + ghost_map[d, v * VARS + w] * planes[w]
                 if d == 0:
-                    state[cur, 1, v, 0] = ghost
+                    state[k, 1, v, 0] = ghost
                 else:
-                    state[cur, 0, v, depth + 1] = ghost
-
-    def advance(k, cur, r, a, last, edge):
+                    state[k, 0, v, depth + 1] = ghost
+
+    def advance(k, r, a, last, edge):
+        tiles = range(ROWS // TILE)
         if edge:
             up_row = corner_in[k, 2 * r:2 * r + 1, :]
             down_row = corner_in[k, 2 * r + 1:2 * r + 2, :]
         else:
             up_row = circ_in[k, r, 0, pl.ds(a, 1), :]
             down_row = circ_in[k, r, 1, pl.ds(a, 1), :]
-        along, around, spread = [], [], []
-        for w in range(VARS):
-            x = state[cur, r, w, a + 1]
-            before, after = state[cur, r, w, a], state[cur, r, w, a + 2]
-            up = jnp.where(row == 0, turned(up_row, LANES - RADIAL - RADIAL * w), turned(x, 1, 0))
-            down = jnp.where(row == ROWS - 1, turned(down_row, -RADIAL * w), turned(x, -1, 0))
-            previous = turned(jnp.where(lane >= LANES - RADIAL, up, x), RADIAL)
-            following = turned(jnp.where(lane < RADIAL, down, x), -RADIAL)
-            if edge:
-                place = r * VARS + w
-                low, high = turned(rim_in[k, 0], -place), turned(rim_in[k, 1], RADIAL - 1 - place)
-            else:
-                low = turned(radial_in[k, r, 0, w], -a)
-                high = turned(radial_in[k, r, 1, w], RADIAL - 1 - a)
-            inner = jnp.where(radial == 0, low, turned(x, 1))
-            outer = jnp.where(radial == RADIAL - 1, high, turned(x, -1))
-            along.append(after - before)
-            around.append(following - previous)
-            spread.append(
-                diffusion * ((after + before) + (following + previous) + (inner + outer) - 6.0 * x)
-            )
-        if last:
-            sum_step = SUM_STEP[3]
-        else:
-            state_step = jnp.where(k == 2, STATE_STEP[2], STATE_STEP[0])
-            sum_step = jnp.where(k == 0, SUM_STEP[0], SUM_STEP[1])
-        new = []
-        for v in range(VARS):
-            rate = spread[v]
+        if not last:
+            step = jnp.where(k == 2, diffusion * STATE_STEP[2], diffusion * STATE_STEP[0])
+        new = [[None] * len(tiles) for _ in range(VARS)]
+        for start in range(0, len(tiles), TOGETHER):
+            chunk = range(start, start + TOGETHER)
+            along, around, rate = {}, {}, {}
             for w in range(VARS):
-                rate = rate + factors[0, r, v * VARS + w] * along[w]
-                rate = rate + factors[1, r, v * VARS + w] * around[w]
-            if last:
-                out[r, v, a] = out[r, v, a] + sum_step * rate
-            else:
-                base = field[r, v, a]
-                total = jnp.where(k == 0, base, out[r, v, a])
-                out[r, v, a] = total + sum_step * rate
-                n = base + state_step * rate
-                state[1 - cur, r, v, a + 1] = n
-                new.append(n)
+                for t in chunk:
+                    lo = t * TILE
+                    here = pl.ds(lo, TILE)
+                    x = state[k, r, w, a + 1, here]
+                    before, after = state[k, r, w, a, here], state[k, r, w, a + 2, here]
+                    if t == 0:
+                        halo = turned(up_row, LANES - RADIAL - RADIAL * w)
+                        up = jnp.where(row8 == 0, halo, turned(x, 1, 0))
+                    else:
+                        up = state[k, r, w, a + 1, pl.ds(lo - 1, TILE)]
+                    if t == tiles[-1]:
+                        halo = turned(down_row, -RADIAL * w)
+                        down = jnp.where(row8 == TILE - 1, halo, turned(x, -1, 0))
+                    else:
+                        down = state[k, r, w, a + 1, pl.ds(lo + 1, TILE)]
+                    previous = turned(jnp.where(at_last, up, x), RADIAL)
+                    following = turned(jnp.where(at_first, down, x), -RADIAL)
+                    if edge:
+                        place = r * VARS + w
+                        low = turned(rim_in[k, 0, here], -place)
+                        high = turned(rim_in[k, 1, here], RADIAL - 1 - place)
+                    else:
+                        low = turned(radial_in[k, r, 0, w, here], -a)
+                        high = turned(radial_in[k, r, 1, w, here], RADIAL - 1 - a)
+                    inner = jnp.where(radial8 == 0, low, turned(x, 1))
+                    outer = jnp.where(radial8 == RADIAL - 1, high, turned(x, -1))
+                    along[w, t] = after - before
+                    around[w, t] = following - previous
+                    rate[w, t] = (
+                        (after + before) + (following + previous) + (inner + outer) - 6.0 * x
+                    )
+            for v in range(VARS):
+                for w in range(VARS):
+                    one, two = factors[0, r, v * VARS + w], factors[1, r, v * VARS + w]
+                    for t in chunk:
+                        rate[v, t] = rate[v, t] + (one * along[w, t] + two * around[w, t])
+                for t in chunk:
+                    here = pl.ds(t * TILE, TILE)
+                    base = state[0, r, v, a + 1, here]
+                    if last:
+                        total = state[1, r, v, a + 1, here] + 2.0 * state[2, r, v, a + 1, here]
+                        total = total + state[3, r, v, a + 1, here] - base
+                        out[r, v, a, here] = (
+                            total * (1.0 / 3.0) + (diffusion * time_step / 6.0) * rate[v, t]
+                        )
+                    else:
+                        n = base + step * rate[v, t]
+                        state[k + 1, r, v, a + 1, here] = n
+                        new[v][t] = n
+                        if not edge:
+                            mine = radial8 == a
+                            radial_out[k + 1, r, 0, v, here] = jnp.where(
+                                mine, turned(n, a - (RADIAL - 1)), radial_out[k + 1, r, 0, v, here]
+                            )
+                            radial_out[k + 1, r, 1, v, here] = jnp.where(
+                                mine, turned(n, a), radial_out[k + 1, r, 1, v, here]
+                            )
+        if not last and not edge:
+            pack_rows(k + 1, r, a, [n[0][:1] for n in new], [n[-1][TILE - 1:] for n in new])
         return new
 
     def stage(k, last=False):
-        cur = k % 2 if isinstance(k, int) else lax.rem(k, 2)
         for r in range(2):
             arrive(sides(k, r), circs(k, r))
 
             def inside(a, carry):
-                new = advance(k, cur, r, a, last, False)
-                if not last:
-                    pack(k + 1, r, a, new)
+                advance(k, r, a, last, False)
                 return carry
 
             lax.fori_loop(r, depth - 1 + r, inside, 0)
             if not last:
                 send(sides(k + 1, r), circs(k + 1, r))
-        for copy in seams(k, cur):
+        for copy in seams(k):
             copy.wait_recv()
-        make_ghosts(k, cur)
+        make_ghosts(k)
         arrive(rims(k), corners(k))
-        planes = [advance(k, cur, r, (depth - 1) * (1 - r), last, True) for r in range(2)]
+        for r in range(2):
+            advance(k, r, (depth - 1) * (1 - r), last, True)
         if not last:
-            for copy in seams(k + 1, 1 - cur):
+            for copy in seams(k + 1):
                 copy.start()
-            pack_edges(k + 1, planes)
+            pack_edges(k + 1)
             send(rims(k + 1), corners(k + 1))
-            own_spectrum(1 - cur)
-        for copy in seams(k, cur):
-            copy.wait_send()
+            own_spectrum(k + 1)
 
     for d, there in enumerate((has_left, has_right)):
 
@@ -508,7 +540,7 @@
                 for r in range(2):
                     radial_in[k, r, d] = jnp.zeros((VARS, ROWS, LANES), jnp.float32)
 
-    for slot in range(2):
+    for slot in range(4):
         for v in range(VARS):
             state[slot, 0, v, 0] = jnp.zeros((ROWS, LANES), jnp.float32)
             state[slot, 1, v, depth + 1] = jnp.zeros((ROWS, LANES), jnp.float32)
@@ -516,6 +548,8 @@
     loads[0].wait()
     loads[1].wait()
     pl.semaphore_wait(barrier, 3)
+    for copy in seams(0):
+        copy.start()
     for r in range(2):
 
         def take_in(a, carry):
@@ -524,12 +558,7 @@
 
         lax.fori_loop(r, depth - 1 + r, take_in, 0)
         send(sides(0, r), circs(0, r))
-        if r == 0:
-            for copy in seams(0, 0):
-                copy.start()
-    pack_edges(
-        0, [[state[0, 0, v, depth] for v in range(VARS)], [state[0, 1, v, 1] for v in range(VARS)]]
-    )
+    pack_edges(0)
     send(rims(0), corners(0))
     for load in loads[2:]:
         load.wait()
@@ -543,6 +572,8 @@
     lax.fori_loop(0, 3, early, 0)
     stage(3, last=True)
     for k in range(4):
+        for copy in seams(k):
+            copy.wait_send()
         for r in range(2):
             sent(sides(k, r), circs(k, r))
         sent(rims(k), corners(k))
@@ -561,14 +592,14 @@
         grid, *small, mode_count, section_offset, mode_source, mode_target,
         jnp.asarray(forward), jnp.asarray(inverse),
     ]
-    places = [pltpu.VMEM] + [pltpu.SMEM] * 6 + [pltpu.VMEM] * 4
+    places = [pltpu.SMEM] * 6 + [pltpu.VMEM] * 4
     result = pl.pallas_call(
         step_kernel,
         out_shape=jax.ShapeDtypeStruct(grid.shape, jnp.float32),
         in_specs=[pl.BlockSpec(memory_space=pltpu.HBM)] * len(args),
         out_specs=pl.BlockSpec(memory_space=pltpu.VMEM),
-        scratch_shapes=[place(x.shape, x.dtype) for place, x in zip(places, args)] + [
-            pltpu.VMEM((2, 2, VARS, depth + 2) + plane, jnp.float32),
+        scratch_shapes=[place(x.shape, x.dtype) for place, x in zip(places, args[1:])] + [
+            pltpu.VMEM((4, 2, VARS, depth + 2) + plane, jnp.float32),
             pltpu.VMEM((4, 2, VARS) + plane, jnp.float32),
             pltpu.VMEM((4, 2, 2, VARS) + plane, jnp.float32),
             pltpu.VMEM((4, 2, 2, VARS) + plane, jnp.float32),
@@ -582,8 +613,8 @@
             pltpu.VMEM((4, 2, K, LANES), jnp.float32),
             pltpu.SMEM((2, VARS * VARS), jnp.float32),
             pltpu.VMEM((2 * K, 2 * LANES), jnp.float32),
-            pltpu.SMEM((2, 2, VARS * VARS), jnp.float32),
-            pltpu.SemaphoreType.DMA((len(args) + 2,)),
+            pltpu.VMEM((2, 2, VARS * VARS, TILE, LANES), jnp.float32),
+            pltpu.SemaphoreType.DMA((len(args) + 1,)),
             pltpu.SemaphoreType.DMA((4, 2)),
             pltpu.SemaphoreType.DMA((4, 2)),
             pltpu.SemaphoreType.DMA((4, 2, 2)),

time: 78.5 us -> 75.8 us (0.966)
  Pallas kernels: 72.9 us -> 70.2 us
    pallas_call x1, Pallas kernels: 72.9 us -> 70.2 us  [fast_path(): pl.pallas_call(step_kernel, out_shape=jax.ShapeDtypeStruct(grid.shape, jn...]
where the time goes in v3:
time: 75.8 us; the launch traced here: 75.7 us
  Pallas kernels  70.2 us (93%)
  local copies, waits for them, and re-layouts  5.4 us (7%)
    pallas_call x1, Pallas kernels, fast_path(): pl.pallas_call(step_kernel, out_shape=jax.ShapeDtypeStruct(grid.shape, jn...  70.2 us
    unnamed x1, local copies, waits for them, and re-layouts  5.4 us

profile of v3, /device:TPU:0, one launch (start us, length us, event | category | flops | bytes accessed | tf_op | source)
XLA Modules:
  0.0 75.7 jit_solution(6691736577535083824)
XLA Ops:
  0.0 70.2 %shard_map.109 = f32[2,5,16,32,128]{4,3,2,1,0:T(8,128)} custom-call(f32[2,5,16,32,128]{4,3,2,1,0:T(8,128)} %bitcast.7, f32[5,2,5]{2,1,0:T(2,128)} %bitcast.8, f32[5,2,5]{2,1,0:T(2,128)} %bitcast.9, f32[5,2,5]{2,1,0:T(2,128)} %bitcast.10, f32[5,2,5]{2,1,0:T(2,128)} %bitcast.11, s32[2]{0:T(128)} %count_hbm.1, s32[4]{0:T(128)} %offset_hbm.1, ...), custom_call_target="tpu_custom_call" | custom-call | tf_op jit(solution)/shard_map/pallas_call | solution.py:596
  70.3 5.4 %copy.14 = f32[2,5,16,1,4096]{4,3,2,1,0:T(1,128)} copy(f32[2,5,16,1,4096]{4,3,2,1,0:T(1,128)} %bitcast.6) | data formatting | bytes 5242880

commit v4 on v3

--- a/solution.py
+++ b/solution.py
@@ -524,9 +524,9 @@
         arrive(rims(k), corners(k))
         for r in range(2):
             advance(k, r, (depth - 1) * (1 - r), last, True)
+            if not last:
+                seams(k + 1)[r].start()
         if not last:
-            for copy in seams(k + 1):
-                copy.start()
             pack_edges(k + 1)
             send(rims(k + 1), corners(k + 1))
             own_spectrum(k + 1)

time: 75.8 us -> 76.1 us (level)
  no operation moved by 1% of the time
where the time goes in v4:
time: 76.1 us; the launch traced here: 76 us
  Pallas kernels  70.6 us (93%)
  local copies, waits for them, and re-layouts  5.4 us (7%)
    pallas_call x1, Pallas kernels, fast_path(): pl.pallas_call(step_kernel, out_shape=jax.ShapeDtypeStruct(grid.shape, jn...  70.6 us
    unnamed x1, local copies, waits for them, and re-layouts  5.4 us

profile of v4, /device:TPU:0, one launch (start us, length us, event | category | flops | bytes accessed | tf_op | source)
XLA Modules:
  0.0 76.0 jit_solution(975860380285497340)
XLA Ops:
  0.0 70.6 %shard_map.109 = f32[2,5,16,32,128]{4,3,2,1,0:T(8,128)} custom-call(f32[2,5,16,32,128]{4,3,2,1,0:T(8,128)} %bitcast.7, f32[5,2,5]{2,1,0:T(2,128)} %bitcast.8, f32[5,2,5]{2,1,0:T(2,128)} %bitcast.9, f32[5,2,5]{2,1,0:T(2,128)} %bitcast.10, f32[5,2,5]{2,1,0:T(2,128)} %bitcast.11, s32[2]{0:T(128)} %count_hbm.1, s32[4]{0:T(128)} %offset_hbm.1, ...), custom_call_target="tpu_custom_call" | custom-call | tf_op jit(solution)/shard_map/pallas_call | solution.py:596
  70.6 5.4 %copy.14 = f32[2,5,16,1,4096]{4,3,2,1,0:T(1,128)} copy(f32[2,5,16,1,4096]{4,3,2,1,0:T(1,128)} %bitcast.6) | data formatting | bytes 5242880
